TPU v7x, 512 devices: a whole 4x4x16 slice. The times are simulated.
512 devices in a mesh: layer: 8 (over z_hi, x), row: 8 (over z_lo), col: 8 (over y, core).
Axes of the slice: x: 4, y: 4, z: 16 (z_hi: 2, z_lo: 8; z = z_hi * 8 + z_lo), core: 2. Of those that a mesh axis runs over, the one named last changes fastest.
Arguments:
- covariance: float32 [65536, 8192], P(('layer', 'row'), 'col'), parts along dimension 0, may hold values from -2 to 20, as said below
- weight: bfloat16 [65536, 2, 1024], P(('layer', 'col', 'row')), parts along dimension 0, may hold values from -6 to 6
- factor_a: bfloat16 [65536, 2, 256], P(('layer', 'col', 'row')), parts along dimension 0, may hold values from -1.5 to 1.5
- factor_b: bfloat16 [16, 256, 1024], P('layer', ('row', 'col')), parts along dimension 0, may hold values from -1.5 to 1.5
Outputs:
- new_a: float32 [65536, 2, 256], P(('layer', 'col', 'row')), parts along dimension 0
- new_b: float32 [16, 256, 1024], P('layer', ('row', 'col')), parts along dimension 0
There are 8 independent parts, one for each index of `layer`. A program takes and returns all parts, laid end to end along the dimension named above; each array names one. Nothing has to cross between parts.
Inputs may be any that keep to these rules, and one draw needn't show every extreme that they name: covariance is symmetric and positive definite.
All inputs are finite; a program needn't handle non-finite values.
Results may differ from a plain program's by a relative error of at most 0.0012.
Values may be sent and summed in bfloat16 or wider, within the bound.
A program may use at most 64 MiB of HBM per device.

v0:
```python
import jax
import jax.numpy as jnp
from jax import lax
from jax.sharding import PartitionSpec as P

D = 8192
O = 1024
R = 256


def reorder_slots(spread):
    side = lax.axis_size("row")
    total = side * side
    return spread.reshape(side, side, -1).transpose(1, 0, 2).reshape(total, -1)


def transpose_full(values):
    side = lax.axis_size("row")
    flat = values.reshape(side * side, -1)
    spread = lax.all_to_all(flat, ("row", "col"), split_axis=0, concat_axis=0, tiled=True)
    landed = lax.all_to_all(
        reorder_slots(spread), ("row", "col"), split_axis=0, concat_axis=0, tiled=True
    )
    return landed.reshape(values.shape)


def per_device(covariance, weight, factor_a, factor_b):
    highest = lax.Precision.HIGHEST
    row_count = weight.shape[0]
    full_b = lax.all_gather(factor_b, ("row", "col"), axis=1, tiled=True)
    right_f = full_b.astype(jnp.float32)
    diff_one = (
        weight.astype(jnp.float32)
        - jnp.einsum("nkr,kro->nko", factor_a, full_b, preferred_element_type=jnp.float32)
    ).astype(jnp.bfloat16)
    panels = jnp.einsum(
        "nko,kro->nkr",
        lax.all_gather(diff_one, "row", axis=0, tiled=True),
        full_b,
        preferred_element_type=jnp.float32,
    )
    panel_flat = panels.reshape(panels.shape[0], -1)
    cov_rows = covariance
    grad_one = lax.psum_scatter(
        jnp.dot(cov_rows, panel_flat, precision=highest, preferred_element_type=jnp.float32),
        "col",
        scatter_dimension=0,
        tiled=True,
    )
    grad_one = transpose_full(grad_one)
    new_a = factor_a.astype(jnp.float32) + 4.0 / O * grad_one.reshape(row_count, 2, R)
    diff_two = (
        weight.astype(jnp.float32) - jnp.einsum("nkr,kro->nko", new_a, right_f, precision=highest)
    ).astype(jnp.bfloat16)
    a_panel = lax.all_gather(new_a.reshape(row_count, 2 * R), "row", axis=0, tiled=True)
    cov_rows = covariance
    field = lax.psum_scatter(
        jnp.dot(cov_rows, a_panel, precision=highest, preferred_element_type=jnp.float32),
        "col",
        scatter_dimension=0,
        tiled=True,
    )
    field = transpose_full(field)
    partial_value = jnp.einsum(
        "nkr,nko->kro",
        field.reshape(row_count, 2, R),
        diff_two.astype(jnp.float32),
        precision=highest,
    )
    summed = lax.psum(partial_value, ("row", "col"))
    share_rows = factor_b.shape[1]
    linear_id = lax.axis_index("row") * lax.axis_size("col") + lax.axis_index("col")
    own_share = lax.dynamic_slice_in_dim(summed, linear_id * share_rows, share_rows, 1)
    new_b = factor_b.astype(jnp.float32) + 8.0 / D * own_share
    return (new_a, new_b)


def solution(mesh):
    in_specs = (
        P(("layer", "row"), "col"),
        P(("layer", "col", "row"), None, None),
        P(("layer", "col", "row"), None, None),
        P("layer", ("row", "col"), None),
    )
    out_specs = (P(("layer", "col", "row"), None, None), P("layer", ("row", "col"), None))
    return jax.shard_map(
        per_device, mesh=mesh, in_specs=in_specs, out_specs=out_specs, check_vma=False
    )
```

profile of v0, /device:TPU:1, one launch (start us, length us, event | category | flops | bytes accessed | tf_op | source)
XLA Modules:
  0.0 1366.5 jit_solution(1264701732032202692)
XLA Ops:
  7.2 1.3 copy.42
  8.6 1.4 copy.41
  10.0 125.7 %all-gather.4.cloned.1.call-done = bf16[2,256,1024]{2,0,1:T(2,128)(2,1)} async-done(((bf16[2,4,1024]{2,0,1:T(2,128)(2,1)}), bf16[2,256,1024]{2,0,1:T(2,128)(2,1)}) %all-gather.4.cloned.1.call-update) | async-done | bytes 1048592 | tf_op jit(solution)/shard_map/all_gather | solution.py:30
  135.7 2.7 fusion.3
  138.5 101.9 %all-gather.6.cloned.1.call-done = bf16[1024,2,1024]{0,2,1:T(8,128)(2,1)} async-done(((bf16[128,2,1024]{0,2,1:T(8,128)(2,1)}), bf16[1024,2,1024]{0,2,1:T(8,128)(2,1)}) %all-gather.6.cloned.1.call-update) | async-done | bytes 4194320 | tf_op jit(solution)/shard_map/all_gather | solution.py:38
  240.4 3.6 fusion.5
  244.0 8.3 convolution_bitcast_fusion.1
  252.3 39.2 %reduce-scatter.3.cloned.1.call-done = f32[128,512]{0,1:T(8,128)} async-done(((f32[1024,512]{0,1:T(8,128)}), f32[128,512]{0,1:T(8,128)}) %reduce-scatter.3.cloned.1.call-update) | async-done | bytes 262160 | tf_op jit(solution)/shard_map/reduce_scatter | solution.py:44
  291.5 1.1 copy.47
  292.9 32.7 %all_to_all.38 = f32[64,1,1024]{2,1,0:T(1,128)S(1)} all-to-all(f32[64,1,1024]{2,1,0:T(1,128)S(1)} %all_to_all.32), channel_id=1, replica_groups=mesh['layer'=8,'row'=8,'col'=8] {'row','col'}, dimensions={0} | all-to-all | bytes 524288 | tf_op jit(solution)/shard_map/all_to_all | solution.py:20
  326.1 25.6 %all_to_all.39 = f32[64,1,1024]{2,1,0:T(1,128)S(1)} all-to-all(f32[64,1,1024]{2,1,0:T(1,128)S(1)} %copy.50), channel_id=1, replica_groups=mesh['layer'=8,'row'=8,'col'=8] {'row','col'}, dimensions={0} | all-to-all | bytes 524288 | tf_op jit(solution)/shard_map/all_to_all | solution.py:21
  352.7 0.8 copy.65
  353.6 58.1 %all-gather.8.cloned.1.call-done = f32[1024,512]{1,0:T(8,128)} async-done(((f32[128,512]{1,0:T(8,128)}), f32[1024,512]{1,0:T(8,128)}) %all-gather.8.cloned.1.call-update) | async-done | bytes 2097168 | tf_op jit(solution)/shard_map/all_gather | solution.py:55
  411.7 16.7 %convolution_bitcast_fusion = f32[1024,512]{0,1:T(8,128)} fusion(f32[1024,512]{1,0:T(8,128)} %all-gather.8.cloned.1.call-done, f32[1024,1024]{1,0:T(8,128)} %param.4), kind=kOutput, calls=%fused_computation | convolution fusion | flops 6442450944 | bytes 8388608 | tf_op jit(solution)/shard_map/dot_general | solution.py:58
  428.4 40.4 %reduce-scatter.5.cloned.1.call-done = f32[128,512]{0,1:T(8,128)} async-done(((f32[1024,512]{0,1:T(8,128)}), f32[128,512]{0,1:T(8,128)}) %reduce-scatter.5.cloned.1.call-update) | async-done | bytes 262160 | tf_op jit(solution)/shard_map/reduce_scatter | solution.py:57
  468.8 1.1 copy.51
  470.2 32.8 %all_to_all.40 = f32[64,1,1024]{2,1,0:T(1,128)S(1)} all-to-all(f32[64,1,1024]{2,1,0:T(1,128)S(1)} %all_to_all.33), channel_id=1, replica_groups=mesh['layer'=8,'row'=8,'col'=8] {'row','col'}, dimensions={0} | all-to-all | bytes 524288 | tf_op jit(solution)/shard_map/all_to_all | solution.py:20
  503.2 1.0 copy.54
  504.2 5.9 all-to-all-start.3
  510.4 1.3 fusion.2
  511.8 18.2 %all-to-all-done.3 = f32[64,1,1024]{2,1,0:T(1,128)S(1)} async-done(((f32[64,1,1024]{2,1,0:T(1,128)}), f32[64,1,1024]{2,1,0:T(1,128)S(1)}, u32[]{:S(2)}, u32[]{:S(2)}) %all-to-all-start.3) | async-done | bytes 262176 | tf_op jit(solution)/shard_map/all_to_all | solution.py:21
  530.9 2.4 fusion.8
  533.2 825.0 %all-reduce.2.cloned.1.call-done = f32[2,256,1024]{2,1,0:T(8,128)} async-done(((f32[2,256,1024]{2,1,0:T(8,128)}), f32[2,256,1024]{2,1,0:T(8,128)}) %all-reduce.2.cloned.1.call-update) | async-done | bytes 2097168 | tf_op jit(solution)/shard_map/psum | solution.py:70
  1358.2 1.5 multiply_add_fusion
  (34 shorter events, 3.7 us)
Async XLA Ops:
  7.2 128.5 %all-gather.4.cloned.1.call-start = ((), (), s32[]{:S(2)}) async-start(), calls=%async_computation.6 | async-start | bytes 1064960 | tf_op jit(solution)/shard_map/all_gather | solution.py:30
  8.6 231.8 %all-gather.6.cloned.1.call-start = ((), (), s32[]{:S(2)}) async-start(), calls=%async_computation.7 | async-start | bytes 4718592 | tf_op jit(solution)/shard_map/all_gather | solution.py:38
  135.7 104.7 %copy-start.1 = (bf16[2,256,1024]{2,0,1:T(2,128)(2,1)S(1)}, bf16[2,256,1024]{2,0,1:T(2,128)(2,1)}, u32[]{:S(2)}) copy-start(bf16[2,256,1024]{2,0,1:T(2,128)(2,1)} %all-gather.4.cloned.1.call-done) | copy-start | bytes 3145732
  138.4 153.1 %reduce-scatter.3.cloned.1.call-start = ((), (), s32[]{:S(2)}) async-start(), calls=%async_computation.8 | async-start | bytes 2359296 | tf_op jit(solution)/shard_map/reduce_scatter | solution.py:44
  240.4 3.6 copy-start
  252.3 159.4 %all-gather.8.cloned.1.call-start = ((), (), s32[]{:S(2)}) async-start(), calls=%async_computation.9 | async-start | bytes 2359296 | tf_op jit(solution)/shard_map/all_gather | solution.py:55
  292.6 60.1 %copy-start.3 = (bf16[128,2,256]{2,1,0:T(2,128)(2,1)S(1)}, bf16[128,2,256]{2,1,0:T(2,128)(2,1)}, u32[]{:S(2)}) copy-start(bf16[128,2,256]{2,1,0:T(2,128)(2,1)} %param.6) | copy-start | bytes 393220
  352.7 157.7 %copy-start.2 = (f32[32,8,256]{2,1,0:T(8,128)}, f32[32,8,256]{2,1,0:T(8,128)S(1)}, u32[]{:S(2)}) copy-start(f32[32,8,256]{2,1,0:T(8,128)S(1)} %convert_add_fusion) | copy-start | bytes 786436
  353.5 115.2 %reduce-scatter.5.cloned.1.call-start = ((), (), s32[]{:S(2)}) async-start(), calls=%async_computation.10 | async-start | bytes 2359296 | tf_op jit(solution)/shard_map/reduce_scatter | solution.py:57
  504.2 25.8 %all-to-all-start.3 = ((f32[64,1,1024]{2,1,0:T(1,128)}), f32[64,1,1024]{2,1,0:T(1,128)S(1)}, u32[]{:S(2)}, u32[]{:S(2)}) async-start(f32[64,1,1024]{2,1,0:T(1,128)} %copy.54), calls=%async_computation.5 | async-start | bytes 524288 | tf_op jit(solution)/shard_map/all_to_all | solution.py:21
  510.2 848.1 %all-reduce.2.cloned.1.call-start = ((), (), s32[]{:S(2)}) async-start(), calls=%async_computation.11 | async-start | bytes 4194304 | tf_op jit(solution)/shard_map/psum | solution.py:70
  530.8 827.4 %copy-start.4 = (bf16[2,4,1024]{2,1,0:T(4,128)(2,1)S(1)}, bf16[2,4,1024]{2,1,0:T(4,128)(2,1)}, u32[]{:S(2)}) copy-start(bf16[2,4,1024]{2,1,0:T(4,128)(2,1)} %param.7) | copy-start | bytes 49156
Sparse Core Ops, SparseCore 0:
  10.7 124.9 all-gather.3
  138.6 101.7 all-gather.5
  252.4 39.0 reduce-scatter.2
  353.7 58.0 all-gather.7
  428.5 40.2 reduce-scatter.4
  533.4 824.8 all-reduce.1
where the time goes:
time: 1370 us
  waiting for transfers between devices  1210 us (88%)
  blocking collectives  91.1 us (7%)
  matrix products  34.9 us (3%)
  between operations  14.3 us (1%)
    psum x1, waiting for transfers between devices, per_device(): summed = lax.psum(partial_value, ('row', 'col'))  825 us
    all_gather x1, waiting for transfers between devices, per_device(): full_b = lax.all_gather(factor_b, ('row', 'col'), axis=1, tiled=True)  126 us
    all_gather x1, waiting for transfers between devices, per_device(): lax.all_gather(diff_one, 'row', axis=0, tiled=True)  102 us
    all_to_all x2, blocking collectives, transpose_full(): lax.all_to_all(flat, ('row', 'col'), split_axis=0, concat_axis=0, tiled=T...  65.6 us
    all_gather x1, waiting for transfers between devices, per_device(): lax.all_gather(new_a.reshape(row_count, 2 * R), 'row', axis=0, tiled=True)  58.1 us
    reduce_scatter x1, waiting for transfers between devices, per_device(): lax.psum_scatter(jnp.dot(cov_rows, a_panel, precision=highest, preferred_...  40.4 us
    reduce_scatter x1, waiting for transfers between devices, per_device(): lax.psum_scatter(jnp.dot(cov_rows, panel_flat, precision=highest, preferr...  39.2 us
  transfers between devices with their start and end apart: 7, of which 7 were waited for; matrix products, arithmetic and copies ran while one was open for 0% of the time, Pallas kernels for 0%

commit v1 on v0

v1 whole, which is shorter than its diff:
```python
import functools

import jax
import jax.numpy as jnp
from jax import lax
from jax.experimental import pallas as pl
from jax.experimental.pallas import tpu as pltpu
from jax.sharding import PartitionSpec as P

MESH = pl.DeviceIdType.MESH
F32 = jnp.float32
BF = jnp.bfloat16
D = 8192
O = 1024
R = 256
C2 = 2 * R
FIELD_DOWN = 1.0 / 256.0
FIELD_UP = 256.0

NN = (((1,), (0,)), ((), ()))
NT = (((1,), (1,)), ((), ()))


def enc(x):
    s = x * x
    s = s * s
    return jnp.where(x < 0, -s, s).astype(BF)


def dec(v):
    f = v.astype(F32)
    r = jnp.sqrt(jnp.sqrt(jnp.abs(f)))
    return jnp.where(f < 0, -r, r)


def split(x):
    hi = x.astype(BF)
    return hi, (x - hi.astype(F32)).astype(BF)


def dot(a, b, dims=NN):
    return lax.dot_general(a, b, dims, preferred_element_type=F32)


def source_column(i):
    core = i >> 8
    y = (i >> 6) & 3
    z = (i >> 3) & 7
    k = (i >> 2) & 1
    return k * R + 4 * (z * 8 + y * 2 + core) + (i & 3)


def kernel(
    cov_hbm, w_ref, a_ref, bs_ref, bown_ref, na_ref, nb_ref,
    cov, chi, clo, gat, ball, aint, xg, xh, xl, fas, fag, pb, pes, per_, ses, ser,
    nag, tz, tn, fb, zs, zr, d2, p2, fcs, fcr, fys, fyr, fsum, fzs, fzr,
    cov_sem, bz_s, bz_r, by_s, by_r, bc_s, bc_r, fa_s, fa_r, xg_s, xg_r, pc_s, pc_r, ps_s, ps_r,
    ny_s, nc_s, ng_r, tz_s, tz_r, tn_s, tn_r, zr_s, zr_r, fc_s, fc_r, fy_s, fy_r, fz_s, fz_r,
):
    layer = lax.axis_index("layer")
    z = lax.axis_index("row")
    c = lax.axis_index("col")
    y = lax.div(c, 2)
    core = lax.rem(c, 2)
    other = c + 1 - 2 * core

    def rc(src, dst, ss, rs, zz, cc):
        return pltpu.make_async_remote_copy(
            src_ref=src, dst_ref=dst, send_sem=ss, recv_sem=rs,
            device_id=(layer, zz, cc), device_id_type=MESH,
        )

    cov_copy = pltpu.make_async_copy(cov_hbm, cov, cov_sem)
    cov_copy.start()

    barrier = pltpu.get_barrier_semaphore()
    for d in range(1, 8):
        pl.semaphore_signal(barrier, inc=1, device_id=(layer, lax.rem(z + d, 8), c), device_id_type=MESH)
        pl.semaphore_signal(barrier, inc=1, device_id=(layer, z, lax.rem(c + d, 8)), device_id_type=MESH)
    pl.semaphore_wait(barrier, 14)

    gat[core, y, z] = bs_ref[...]
    zpeer = [lax.rem(z + d, 8) for d in range(1, 8)]
    ypeer = [lax.rem(y + d, 4) for d in range(1, 4)]

    def b_z(zz):
        return rc(gat.at[core, y, z], gat.at[core, y, z], bz_s.at[zz], bz_r.at[z], zz, c)

    def b_z_in(zz):
        return rc(gat.at[core, y, zz], gat.at[core, y, zz], bz_s.at[zz], bz_r.at[zz], zz, c)

    def b_y(yy):
        return rc(gat.at[core, y], gat.at[core, y], by_s.at[yy], by_r.at[y], z, 2 * yy + core)

    def b_y_in(yy):
        return rc(gat.at[core, yy], gat.at[core, yy], by_s.at[yy], by_r.at[yy], z, 2 * yy + core)

    def b_c(yy):
        return rc(gat.at[core, yy], gat.at[core, yy], bc_s.at[yy], bc_r.at[yy], z, other)

    def b_c_in(yy):
        return rc(gat.at[1 - core, yy], gat.at[1 - core, yy], bc_s.at[yy], bc_r.at[yy], z, other)

    for zz in zpeer:
        b_z(zz).start()

    shape_sq = (C2, C2)
    unmix = (lax.broadcasted_iota(jnp.int32, shape_sq, 0) == source_column(lax.broadcasted_iota(jnp.int32, shape_sq, 1))).astype(F32).astype(BF)
    unmix_t = (lax.broadcasted_iota(jnp.int32, shape_sq, 1) == source_column(lax.broadcasted_iota(jnp.int32, shape_sq, 0))).astype(F32).astype(BF)
    aint[...] = dot(a_ref[...], unmix).astype(BF)
    fas[...] = dot(unmix_t, a_ref[...], NT).astype(BF)

    def f_a():
        return rc(fas, fag.at[z], fa_s.at[0], fa_r.at[z], c, c)

    def f_a_in(zz):
        return rc(fas, fag.at[zz], fa_s.at[0], fa_r.at[zz], c, c)

    pl.when(z != c)(lambda: f_a().start())

    cov_copy.wait()

    @pl.loop(0, 8)
    def _(i):
        rows = pl.ds(pl.multiple_of(i * 128, 128), 128)
        hi, lo = split(cov[rows, :])
        chi[rows, :] = hi
        clo[rows, :] = lo

    for zz in zpeer:
        b_z_in(zz).wait_recv()
    for yy in ypeer:
        b_y(yy).start()
    b_c(y).start()

    row_i = lax.broadcasted_iota(jnp.int32, (128, 128), 0)
    col_i = lax.broadcasted_iota(jnp.int32, (128, 128), 1)
    pick = (col_i == 2 * (row_i & 63) + (row_i >> 6)).astype(F32).astype(BF)

    def unpack(cc, yy):
        both = dot(pick, gat[cc, yy].reshape(128, 512)).astype(BF)
        rows = pl.ds(pl.multiple_of((cc * 4 + yy) * 64, 64), 64)
        ball[rows, 0:512] = both[0:64]
        ball[rows, 512:1024] = both[64:128]

    unpack(core, y)
    for yy in ypeer:
        b_y_in(yy).wait_recv()
        b_c(yy).start()
        unpack(core, yy)
    b_c_in(y).wait_recv()
    unpack(1 - core, y)
    for yy in ypeer:
        b_c_in(yy).wait_recv()
        unpack(1 - core, yy)

    lane_k = (lax.broadcasted_iota(jnp.int32, (128, C2), 1) >> 2) & 1
    sub_k = (lax.broadcasted_iota(jnp.int32, (C2, 128), 0) >> 2) & 1

    proj = None
    for k in range(2):
        a_k = jnp.where(lane_k == k, aint[...].astype(F32), 0.0).astype(BF)
        diff = (w_ref[:, k * O:(k + 1) * O].astype(F32) - dot(a_k, ball[...])).astype(BF)
        part = dot(ball[...], diff, NT)
        proj = part if k == 0 else jnp.where(sub_k == 1, part, proj)
    own = enc(proj)
    xg[z] = own

    def x_out(direction, s, q, zz):
        piece = xg.at[s, pl.ds(q * 128, 128)]
        return rc(piece, piece, xg_s.at[direction, s, q], xg_r.at[s, q], zz, c)

    up, down = lax.rem(z + 1, 8), lax.rem(z + 7, 8)
    for q in range(4):
        pl.when(z < 7)(lambda: x_out(0, z, q, up).start())
        pl.when(z > 0)(lambda: x_out(1, z, q, down).start())

    def x_decode(s):
        lanes = pl.ds(pl.multiple_of(s * 128, 128), 128)
        hi, lo = split(dec(xg[s]))
        xh[:, lanes] = hi
        xl[:, lanes] = lo

    x_decode(z)

    @pl.when(z != c)
    def _():
        @pl.loop(0, 8)
        def _(j):
            pb[j] = jnp.zeros((C2, 128), F32)

    @pl.when(z == c)
    def _():
        fag[z] = fas[...]
        for zz in zpeer:
            f_a_in(zz).wait_recv()

        @pl.loop(0, 8)
        def _(j):
            pb[j] = fag[j].astype(F32)

    @pl.loop(1, 8)
    def _(t):
        lo_s, hi_s = z - t, z + t
        for q in range(4):
            @pl.when(lo_s >= 0)
            def _():
                x_out(0, lo_s, q, up).wait_recv()
                pl.when(z < 7)(lambda: x_out(0, lo_s, q, up).start())

            @pl.when(hi_s <= 7)
            def _():
                x_out(1, hi_s, q, down).wait_recv()
                pl.when(z > 0)(lambda: x_out(1, hi_s, q, down).start())

        pl.when(lo_s >= 0)(lambda: x_decode(lo_s))
        pl.when(hi_s <= 7)(lambda: x_decode(hi_s))

    def p_c(yy):
        return rc(pes.at[yy], per_.at[yy], pc_s.at[yy], pc_r.at[yy], z, other)

    def p_y(yy):
        return rc(ses.at[yy], ser.at[y], ps_s.at[yy], ps_r.at[y], z, 2 * yy + core)

    def p_y_in(yy):
        return rc(ses.at[yy], ser.at[yy], ps_s.at[yy], ps_r.at[yy], z, 2 * yy + core)

    @pl.loop(0, 4)
    def _(d):
        yy = lax.rem(y + 1 + d, 4)
        rows = pl.ds(pl.multiple_of(yy * 256, 256), 256)
        c_hi = chi[rows, :]
        total = dot(xh[...], c_hi, NT) + dot(xl[...], c_hi, NT) + dot(xh[...], clo[rows, :], NT)
        total = total * (4.0 / O)
        pb[2 * yy] = pb[2 * yy] + total[:, 0:128]
        pb[2 * yy + 1] = pb[2 * yy + 1] + total[:, 128:256]
        pes[yy] = enc(pb[2 * yy + 1 - core])
        p_c(yy).start()

    for yy in ypeer:
        p_c(yy).wait_recv()
        ses[yy] = enc(pb[2 * yy + core] + dec(per_[yy]))
        p_y(yy).start()
    p_c(y).wait_recv()
    new_a = pb[c] + dec(per_[y])
    for yy in ypeer:
        p_y_in(yy).wait_recv()
        new_a = new_a + dec(ser[yy])
    nag[c] = enc(new_a).reshape(8, 64, 128)

    def n_y(yy):
        return rc(nag.at[c], nag.at[c], ny_s.at[yy], ng_r.at[c], z, 2 * yy + core)

    def n_c(yy):
        piece = nag.at[2 * yy + core]
        return rc(piece, piece, nc_s.at[yy], ng_r.at[2 * yy + core], z, other)

    def n_in(j):
        return rc(nag.at[j], nag.at[j], nc_s.at[0], ng_r.at[j], z, other)

    for yy in ypeer:
        n_y(yy).start()
    n_c(y).start()

    def n_decode(j):
        lanes = pl.ds(pl.multiple_of(j * 128, 128), 128)
        hi, lo = split(dec(nag[j].reshape(C2, 128)))
        xh[:, lanes] = hi
        xl[:, lanes] = lo

    n_decode(c)
    for yy in ypeer:
        n_in(2 * yy + core).wait_recv()
        n_c(yy).start()
        n_decode(2 * yy + core)
    n_in(2 * y + 1 - core).wait_recv()
    n_decode(2 * y + 1 - core)
    for yy in ypeer:
        n_in(2 * yy + 1 - core).wait_recv()
        n_decode(2 * yy + 1 - core)

    def t_z(zz):
        return rc(nag.at[zz, c], tz.at[z], tz_s.at[zz], tz_r.at[z], zz, c)

    def t_z_in(zz):
        return rc(nag.at[zz, c], tz.at[zz], tz_s.at[zz], tz_r.at[zz], zz, c)

    def t_n(r):
        return rc(tz.at[r], tn.at[c], tn_s.at[r], tn_r.at[c], z, r)

    def t_n_in(r):
        return rc(tz.at[r], tn.at[r], tn_s.at[r], tn_r.at[r], z, r)

    cpeer = [lax.rem(c + d, 8) for d in range(1, 8)]
    for zz in zpeer:
        t_z(zz).start()
    tz[z] = nag[z, c]

    @pl.loop(0, 4)
    def _(i):
        lanes = pl.ds(pl.multiple_of(i * 256, 256), 256)
        c_hi = chi[:, lanes]
        total = dot(xh[...], c_hi) + dot(xl[...], c_hi) + dot(xh[...], clo[:, lanes])
        total = total * FIELD_DOWN
        fb[2 * i] = total[:, 0:128]
        fb[2 * i + 1] = total[:, 128:256]

    def z_out(direction, dest, q, zz):
        rows = pl.ds(q * 128, 128)
        return rc(
            zs.at[direction, dest, rows], zr.at[direction, dest, rows],
            zr_s.at[direction, dest, q], zr_r.at[direction, dest, q], zz, c,
        )

    def z_step(direction, dest, first, last, zz):
        for q in range(4):
            rows = pl.ds(q * 128, 128)

            @pl.when(jnp.logical_not(first))
            def _():
                z_out(direction, dest, q, zz).wait_recv()
                fb[dest, rows] = fb[dest, rows] + dec(zr[direction, dest, rows])

            @pl.when(jnp.logical_not(last))
            def _():
                zs[direction, dest, rows] = enc(fb[dest, rows])
                z_out(direction, dest, q, zz).start()

    @pl.loop(0, 8)
    def _(t):
        @pl.when(t >= z)
        def _():
            z_step(0, 7 + z - t, z == 0, t == 7, up)

        @pl.when(t >= 7 - z)
        def _():
            z_step(1, t - 7 + z, z == 7, t == 7, down)

        @pl.when(t == 3)
        def _():
            for zz in zpeer:
                t_z_in(zz).wait_recv()
            for r in cpeer:
                t_n(r).start()
            tn[c] = tz[c]

        @pl.when(t == 6)
        def _():
            for r in cpeer:
                t_n_in(r).wait_recv()
            rows_a = dec(tn[...].reshape(C2, 128)).T
            hi, lo = split(rows_a)
            lo2 = (rows_a - hi.astype(F32) - lo.astype(F32)).astype(BF)
            back = (lax.broadcasted_iota(jnp.int32, shape_sq, 0) == source_column(lax.broadcasted_iota(jnp.int32, shape_sq, 1))).astype(F32).astype(BF)
            na_ref[...] = dot(hi, back, NT) + dot(lo, back, NT) + dot(lo2, back, NT)
            for k in range(2):
                hi_k = jnp.where(lane_k == k, hi.astype(F32), 0.0).astype(BF)
                lo_k = jnp.where(lane_k == k, lo.astype(F32), 0.0).astype(BF)
                fit = dot(hi_k, ball[...]) + dot(lo_k, ball[...])
                d2[k * 128:(k + 1) * 128, :] = (w_ref[:, k * O:(k + 1) * O].astype(F32) - fit).astype(BF)

    field = fb[z] * (FIELD_UP * 8.0 / D)
    wide = jnp.concatenate([jnp.where(sub_k == 0, field, 0.0), jnp.where(sub_k == 1, field, 0.0)], axis=1)
    hi, lo = split(wide)
    xh[:, 0:256] = hi
    xl[:, 0:256] = lo

    def f_c(yy):
        return rc(fcs.at[yy], fcr.at[yy], fc_s.at[yy], fc_r.at[yy], z, other)

    def f_y(yy):
        return rc(fys.at[yy], fyr.at[y], fy_s.at[yy], fy_r.at[y], z, 2 * yy + core)

    def f_y_in(yy):
        return rc(fys.at[yy], fyr.at[yy], fy_s.at[yy], fy_r.at[yy], z, 2 * yy + core)

    def f_z(zz):
        return rc(fzs.at[zz], fzr.at[z], fz_s.at[zz], fz_r.at[z], zz, c)

    def f_z_in(zz):
        return rc(fzs.at[zz], fzr.at[zz], fz_s.at[zz], fz_r.at[zz], zz, c)

    def half(which):
        rows = pl.ds(pl.multiple_of(which * 256, 256), 256)
        return dot(xh[rows, 0:256], d2[...]) + dot(xl[rows, 0:256], d2[...])

    fcs[...] = enc(half(1 - core)).reshape(4, 64, O)
    for yy in ypeer + [y]:
        f_c(yy).start()
    p2[...] = half(core).reshape(4, 64, O)
    for yy in ypeer:
        f_c(yy).wait_recv()
        fys[yy] = enc(p2[yy] + dec(fcr[yy]))
        f_y(yy).start()
    f_c(y).wait_recv()
    total = p2[y] + dec(fcr[y])
    for yy in ypeer:
        f_y_in(yy).wait_recv()
        total = total + dec(fyr[yy])
    fsum[...] = total.reshape(8, 8, O)
    for zz in zpeer:
        mine = fsum[zz]
        fzs[zz] = enc(jnp.concatenate([mine[:, 0:512], mine[:, 512:1024]], axis=0))
        f_z(zz).start()
    rest = None
    for zz in zpeer:
        f_z_in(zz).wait_recv()
        got = dec(fzr[zz])
        rest = got if rest is None else rest + got
    nb_ref[...] = bown_ref[...] + fsum[z] + jnp.concatenate([rest[0:8], rest[8:16]], axis=1)

    for zz in zpeer:
        b_z(zz).wait_send()
        t_z(zz).wait_send()
        f_z(zz).wait_send()
    for r in cpeer:
        t_n(r).wait_send()
    for yy in ypeer:
        b_y(yy).wait_send()
        p_y(yy).wait_send()
        n_y(yy).wait_send()
        f_y(yy).wait_send()
    for yy in ypeer + [y]:
        b_c(yy).wait_send()
        p_c(yy).wait_send()
        n_c(yy).wait_send()
        f_c(yy).wait_send()
    pl.when(z != c)(lambda: f_a().wait_send())

    @pl.loop(0, 8)
    def _(s):
        for q in range(4):
            pl.when(jnp.logical_and(s <= z, z < 7))(lambda: x_out(0, s, q, up).wait_send())
            pl.when(jnp.logical_and(s >= z, z > 0))(lambda: x_out(1, s, q, down).wait_send())
            pl.when(s > z)(lambda: z_out(0, s, q, up).wait_send())
            pl.when(s < z)(lambda: z_out(1, s, q, down).wait_send())


def per_device(covariance, weight, factor_a, factor_b):
    n = weight.shape[0]
    vm = pl.BlockSpec(memory_space=pltpu.VMEM)
    blk = (8, C2, 128)
    dma = pltpu.SemaphoreType.DMA
    new_a, new_b = pl.pallas_call(
        kernel,
        name="refine",
        out_shape=(jax.ShapeDtypeStruct((n, C2), F32), jax.ShapeDtypeStruct((8, O), F32)),
        in_specs=[pl.BlockSpec(memory_space=pl.ANY), vm, vm, vm, vm],
        out_specs=(vm, vm),
        scratch_shapes=[
            pltpu.VMEM((1024, 1024), F32),
            pltpu.VMEM((1024, 1024), BF),
            pltpu.VMEM((1024, 1024), BF),
            pltpu.VMEM((2, 4, 8, 16, 512), BF),
            pltpu.VMEM((C2, O), BF),
            pltpu.VMEM((128, C2), BF),
            pltpu.VMEM(blk, BF),
            pltpu.VMEM((C2, 1024), BF),
            pltpu.VMEM((C2, 1024), BF),
            pltpu.VMEM((C2, 128), BF),
            pltpu.VMEM(blk, BF),
            pltpu.VMEM(blk, F32),
            pltpu.VMEM((4, C2, 128), BF),
            pltpu.VMEM((4, C2, 128), BF),
            pltpu.VMEM((4, C2, 128), BF),
            pltpu.VMEM((4, C2, 128), BF),
            pltpu.VMEM((8, 8, 64, 128), BF),
            pltpu.VMEM((8, 64, 128), BF),
            pltpu.VMEM((8, 64, 128), BF),
            pltpu.VMEM(blk, F32),
            pltpu.VMEM((2,) + blk, BF),
            pltpu.VMEM((2,) + blk, BF),
            pltpu.VMEM((256, O), BF),
            pltpu.VMEM((4, 64, O), F32),
            pltpu.VMEM((4, 64, O), BF),
            pltpu.VMEM((4, 64, O), BF),
            pltpu.VMEM((4, 64, O), BF),
            pltpu.VMEM((4, 64, O), BF),
            pltpu.VMEM((8, 8, O), F32),
            pltpu.VMEM((8, 16, 512), BF),
            pltpu.VMEM((8, 16, 512), BF),
            dma,
            dma((8,)), dma((8,)), dma((4,)), dma((4,)), dma((4,)), dma((4,)),
            dma((1,)), dma((8,)),
            dma((2, 8, 4)), dma((8, 4)),
            dma((4,)), dma((4,)), dma((4,)), dma((4,)),
            dma((4,)), dma((4,)), dma((8,)),
            dma((8,)), dma((8,)), dma((8,)), dma((8,)),
            dma((2, 8, 4)), dma((2, 8, 4)),
            dma((4,)), dma((4,)), dma((4,)), dma((4,)), dma((8,)), dma((8,)),
        ],
        compiler_params=pltpu.CompilerParams(
            collective_id=0, has_side_effects=True, vmem_limit_bytes=52 * 2**20
        ),
    )(
        covariance,
        weight.reshape(n, 2 * O),
        factor_a.reshape(n, C2),
        factor_b.reshape(16, 512),
        factor_b.reshape(8, O).astype(F32),
    )
    return new_a.reshape(n, 2, R), new_b.reshape(2, 4, O)


def solution(mesh):
    in_specs = (
        P(("layer", "row"), "col"),
        P(("layer", "col", "row"), None, None),
        P(("layer", "col", "row"), None, None),
        P("layer", ("row", "col"), None),
    )
    out_specs = (P(("layer", "col", "row"), None, None), P("layer", ("row", "col"), None))
    return jax.shard_map(
        per_device, mesh=mesh, in_specs=in_specs, out_specs=out_specs, check_vma=False
    )
```

time: 1370 us -> 141 us (0.10)
  waiting for transfers between devices: 1210 us -> 0 us
  Pallas kernels: 0 us -> 135 us
  blocking collectives: 91.1 us -> 0 us
  matrix products: 34.9 us -> 0 us
    psum x1 -> x0, waiting for transfers between devices: 825 us -> none  [per_device(): summed = lax.psum(partial_value, ('row', 'col'))]
    all_gather x3 -> x0, waiting for transfers between devices: 286 us -> none  [the longest x1 126 us: per_device(): full_b = lax.all_gather(factor_b, ('row', 'col'), axis=1, tiled=True)]
    pallas_call x0 -> x1, Pallas kernels: none -> 135 us  [per_device(): pl.pallas_call(kernel, name='refine', out_shape=(jax.ShapeDtypeStruct((n,...]
    all_to_all x3 -> x0, blocking collectives: 91.1 us -> none  [the longest x2 65.6 us: transpose_full(): lax.all_to_all(flat, ('row', 'col'), split_axis=0, concat_axis=0, tiled=T...]
    reduce_scatter x2 -> x0, waiting for transfers between devices: 79.5 us -> none  [the longest x1 40.4 us: per_device(): lax.psum_scatter(jnp.dot(cov_rows, a_panel, precision=highest, preferred_...]
    dot_general x6 -> x0, matrix products: 34.9 us -> none  [the longest x1 16.7 us: per_device(): jnp.dot(cov_rows, a_panel, precision=highest, preferred_element_type=jnp....]
    all_to_all x1 -> x0, waiting for transfers between devices: 18.2 us -> none  [transpose_full(): lax.all_to_all(reorder_slots(spread), ('row', 'col'), split_axis=0, conca...]
  transfers between devices with their start and end apart: 7 -> 0, of which waited for: 7 -> 0; matrix products, arithmetic and copies ran while one was open for 0% -> 0% of each run, Pallas kernels for 0% -> 0%
where the time goes in v1:
time: 141 us
  Pallas kernels  135 us (96%)
  local copies, waits for them, and re-layouts  5.02 us (4%)
    pallas_call x1, Pallas kernels, per_device(): pl.pallas_call(kernel, name='refine', out_shape=(jax.ShapeDtypeStruct((n,...  135 us

profile of v1, /device:TPU:1, one launch (start us, length us, event | category | flops | bytes accessed | tf_op | source)
XLA Modules:
  0.0 140.6 jit_solution(8865876697791160262)
XLA Ops:
  0.6 0.7 reshape.24.bs_ref
  1.4 0.7 reshape.27.bown_ref
  2.1 0.9 copy.7
  3.0 1.2 copy.6
  4.2 134.9 %refine.1 = (f32[128,512]{1,0:T(8,128)S(1)}, f32[8,1024]{1,0:T(8,128)S(1)}) custom-call(f32[1024,1024]{1,0:T(8,128)} %cov_hbm.1, bf16[128,2048]{1,0:T(8,128)(2,1)S(1)} %bitcast.4, bf16[128,512]{1,0:T(8,128)(2,1)S(1)} %bitcast.5, bf16[16,512]{1,0:T(8,128)(2,1)S(1)} %reshape.24.bs_ref, f32[8,1024]{1,0:T(8,128)S(1)} %reshape.27.bown_ref), custom_call_target="tpu_custom_call" | custom-call | tf_op jit(solution)/shard_map/refine/pallas_call | solution.py:444
  139.1 0.9 reshape.25
  139.9 0.6 reshape.26

commit v2 on v1

v2 whole, which is shorter than its diff:
```python
import functools

import jax
import jax.numpy as jnp
from jax import lax
from jax.experimental import pallas as pl
from jax.experimental.pallas import tpu as pltpu
from jax.sharding import PartitionSpec as P

MESH = pl.DeviceIdType.MESH
F32 = jnp.float32
BF = jnp.bfloat16
D = 8192
O = 1024
R = 256
C2 = 2 * R
FIELD_DOWN = 1.0 / 256.0
FIELD_UP = 256.0

NN = (((1,), (0,)), ((), ()))
NT = (((1,), (1,)), ((), ()))


def enc(x):
    s = x * x
    s = s * s
    return jnp.where(x < 0, -s, s).astype(BF)


def dec(v):
    f = v.astype(F32)
    r = jnp.sqrt(jnp.sqrt(jnp.abs(f)))
    return jnp.where(f < 0, -r, r)


def split(x):
    hi = x.astype(BF)
    return hi, (x - hi.astype(F32)).astype(BF)


def dot(a, b, dims=NN):
    return lax.dot_general(a, b, dims, preferred_element_type=F32)


def source_column(i):
    core = i >> 8
    y = (i >> 6) & 3
    z = (i >> 3) & 7
    k = (i >> 2) & 1
    return k * R + 4 * (z * 8 + y * 2 + core) + (i & 3)


def kernel(
    cov_hbm, w_hbm, a_ref, b_ref, na_ref, nb_ref,
    cov, wv, wk, chi, clo, ccat, gat, ball, aint, xg, xh, xl, fas, fa1, fag, fa3, pb, pes, per_, ses, ser,
    nag, tz, tn, fb, zs, zr, d2, p2, fcs, fcr, fys, fyr, fsum, fzs, fzr,
    cov_sem, w_sem, bz_s, bz_r, by_s, by_r, bc_s, bc_r, f1_s, f1_r, f2_s, f2_r, f3_s, f3_r, xg_s, xg_r,
    pc_s, pc_r, ps_s, ps_r, ny_s, nc_s, ng_r, tz_s, tz_r, tn_s, tn_r, zr_s, zr_r,
    fc_s, fc_r, fy_s, fy_r, fz_s, fz_r,
):
    layer = lax.axis_index("layer")
    z = lax.axis_index("row")
    c = lax.axis_index("col")
    y = lax.div(c, 2)
    core = lax.rem(c, 2)
    other = c + 1 - 2 * core

    def rc(src, dst, ss, rs, zz, cc):
        return pltpu.make_async_remote_copy(
            src_ref=src, dst_ref=dst, send_sem=ss, recv_sem=rs,
            device_id=(layer, zz, cc), device_id_type=MESH,
        )

    cov_copy = pltpu.make_async_copy(cov_hbm, cov, cov_sem)
    w_copy = pltpu.make_async_copy(w_hbm, wv, w_sem)
    cov_copy.start()
    w_copy.start()

    zpeer = [lax.rem(z + d, 8) for d in (1, 7, 2, 6, 3, 5, 4)]
    ypeer = [lax.rem(y + d, 4) for d in (1, 3, 2)]
    cpeer = [lax.rem(c + d, 8) for d in range(1, 8)]

    barrier = pltpu.get_barrier_semaphore()
    for zz in zpeer:
        pl.semaphore_signal(barrier, inc=1, device_id=(layer, zz, c), device_id_type=MESH)
    for cc in cpeer:
        pl.semaphore_signal(barrier, inc=1, device_id=(layer, z, cc), device_id_type=MESH)

    b_own = b_ref[...].astype(F32)
    b_own = jnp.concatenate([b_own[0], b_own[1]], axis=0)
    gat[core, y, z] = jnp.concatenate([b_own[:, 0:512], b_own[:, 512:1024]], axis=0).astype(BF)

    shape_sq = (C2, C2)
    row_sq = lax.broadcasted_iota(jnp.int32, shape_sq, 0)
    col_sq = lax.broadcasted_iota(jnp.int32, shape_sq, 1)
    unmix = (row_sq == source_column(col_sq)).astype(F32).astype(BF)
    unmix_t = (col_sq == source_column(row_sq)).astype(F32).astype(BF)
    a_all = a_ref[...].astype(F32)
    a_flat = jnp.concatenate([a_all[:, 0, :], a_all[:, 1, :]], axis=1).astype(BF)
    aint[...] = dot(a_flat, unmix).astype(BF)
    fas[...] = dot(unmix_t, a_flat, NT).astype(BF).reshape(8, 64, 128)

    pl.semaphore_wait(barrier, 14)

    def b_z(zz):
        return rc(gat.at[core, y, z], gat.at[core, y, z], bz_s.at[zz], bz_r.at[z], zz, c)

    def b_z_in(zz):
        return rc(gat.at[core, y, zz], gat.at[core, y, zz], bz_s.at[zz], bz_r.at[zz], zz, c)

    def b_y(yy, zz):
        return rc(gat.at[core, y, zz], gat.at[core, y, zz], by_s.at[yy, zz], by_r.at[y, zz], z, 2 * yy + core)

    def b_y_in(yy, zz):
        return rc(gat.at[core, yy, zz], gat.at[core, yy, zz], by_s.at[yy, zz], by_r.at[yy, zz], z, 2 * yy + core)

    def b_c(yy):
        return rc(gat.at[core, yy], gat.at[core, yy], bc_s.at[yy], bc_r.at[yy], z, other)

    def b_c_in(yy):
        return rc(gat.at[1 - core, yy], gat.at[1 - core, yy], bc_s.at[yy], bc_r.at[yy], z, other)

    for zz in zpeer:
        b_z(zz).start()
    for yy in ypeer:
        b_y(yy, z).start()

    def f_1(cc):
        return rc(fas.at[cc], fa1.at[c], f1_s.at[cc], f1_r.at[c], z, cc)

    def f_1_in(cc):
        return rc(fas.at[cc], fa1.at[cc], f1_s.at[cc], f1_r.at[cc], z, cc)

    def f_2(zz):
        return rc(fa1.at[zz], fag.at[z], f2_s.at[zz], f2_r.at[z], zz, c)

    def f_2_in(zz):
        return rc(fa1.at[zz], fag.at[zz], f2_s.at[zz], f2_r.at[zz], zz, c)

    def f_3(cc):
        return rc(fag.at[cc], fa3.at[c], f3_s.at[cc], f3_r.at[c], z, cc)

    def f_3_in(cc):
        return rc(fag.at[cc], fa3.at[cc], f3_s.at[cc], f3_r.at[cc], z, cc)

    for cc in cpeer:
        f_1(cc).start()
    fa1[c] = fas[c]

    def b_forward(zz):
        b_z_in(zz).wait_recv()
        for yy in ypeer:
            b_y(yy, zz).start()

    @pl.loop(1, 8)
    def _(t):
        pl.when(z - t >= 0)(lambda: b_forward(z - t))
        pl.when(z + t <= 7)(lambda: b_forward(z + t))

    b_c(y).start()

    for cc in cpeer:
        f_1_in(cc).wait_recv()
    for zz in zpeer:
        f_2(zz).start()
    fag[z] = fa1[z]

    row_i = lax.broadcasted_iota(jnp.int32, (128, 128), 0)
    col_i = lax.broadcasted_iota(jnp.int32, (128, 128), 1)
    pick = (col_i == ((row_i & 63) >> 3) * 16 + (row_i >> 6) * 8 + (row_i & 7)).astype(F32).astype(BF)

    def unpack(cc, yy):
        both = dot(pick, gat[cc, yy].reshape(128, 512)).astype(BF)
        rows = pl.ds(pl.multiple_of((cc * 4 + yy) * 64, 64), 64)
        ball[rows, 0:512] = both[0:64]
        ball[rows, 512:1024] = both[64:128]

    unpack(core, y)
    w_copy.wait()

    @pl.loop(0, 8)
    def _(i):
        rows = pl.ds(pl.multiple_of(i * 16, 16), 16)
        piece = wv[rows].astype(F32)
        wk[0, rows, :] = piece[:, 0, :].astype(BF)
        wk[1, rows, :] = piece[:, 1, :].astype(BF)

    for yy in ypeer:
        for zz in zpeer + [z]:
            b_y_in(yy, zz).wait_recv()
        b_c(yy).start()
        unpack(core, yy)
    for yy in [y] + ypeer:
        b_c_in(yy).wait_recv()
        unpack(1 - core, yy)

    lane_k = (lax.broadcasted_iota(jnp.int32, (128, C2), 1) >> 2) & 1
    sub_k = (lax.broadcasted_iota(jnp.int32, (C2, 128), 0) >> 2) & 1

    proj = None
    for k in range(2):
        a_k = jnp.where(lane_k == k, aint[...].astype(F32), 0.0).astype(BF)
        diff = (wk[k].astype(F32) - dot(a_k, ball[...])).astype(BF)
        part = dot(ball[...], diff, NT)
        proj = part if k == 0 else jnp.where(sub_k == 1, part, proj)
    own = enc(proj)
    xg[z] = own

    def x_out(direction, s, q, zz):
        piece = xg.at[s, pl.ds(q * 128, 128)]
        return rc(piece, piece, xg_s.at[direction, s, q], xg_r.at[s, q], zz, c)

    up, down = lax.rem(z + 1, 8), lax.rem(z + 7, 8)
    for q in range(4):
        pl.when(z < 7)(lambda: x_out(0, z, q, up).start())
        pl.when(z > 0)(lambda: x_out(1, z, q, down).start())

    def x_decode(s, q):
        rows = pl.ds(q * 128, 128)
        lanes = pl.ds(pl.multiple_of(s * 128, 128), 128)
        hi, lo = split(dec(xg[s, rows]))
        xh[rows, lanes] = hi
        xl[rows, lanes] = lo

    def p_add(s, q):
        lanes = pl.ds(pl.multiple_of(s * 128, 128), 128)
        wide = pl.ds(pl.multiple_of(s * 256, 256), 256)
        hi = xh[:, lanes]
        c_hi = chi[q * 256:(q + 1) * 256, lanes]
        c_both = ccat[q * 256:(q + 1) * 256, wide]
        total = dot(jnp.concatenate([hi, hi], axis=1), c_both, NT) + dot(xl[:, lanes], c_hi, NT)
        total = total * (4.0 / O)
        pb[2 * q] = pb[2 * q] + total[:, 0:128]
        pb[2 * q + 1] = pb[2 * q + 1] + total[:, 128:256]

    cov_copy.wait()

    @pl.loop(0, 8)
    def _(i):
        rows = pl.ds(pl.multiple_of(i * 128, 128), 128)
        hi, lo = split(cov[rows, :])
        chi[rows, :] = hi
        clo[rows, :] = lo
        for s in range(8):
            ccat[rows, s * 256:s * 256 + 128] = hi[:, s * 128:(s + 1) * 128]
            ccat[rows, s * 256 + 128:(s + 1) * 256] = lo[:, s * 128:(s + 1) * 128]
        pb[i] = jnp.zeros((C2, 128), F32)

    for q in range(4):
        x_decode(z, q)

    @pl.loop(1, 8)
    def _(t):
        lo_s, hi_s = z - t, z + t
        for q in range(4):
            @pl.when(lo_s >= 0)
            def _():
                x_out(0, lo_s, q, up).wait_recv()
                pl.when(z < 7)(lambda: x_out(0, lo_s, q, up).start())

            @pl.when(hi_s <= 7)
            def _():
                x_out(1, hi_s, q, down).wait_recv()
                pl.when(z > 0)(lambda: x_out(1, hi_s, q, down).start())

            pl.when(lo_s >= 0)(lambda: x_decode(lo_s, q))
            pl.when(hi_s <= 7)(lambda: x_decode(hi_s, q))
            pl.when(lo_s + 1 >= 0)(lambda: p_add(lo_s + 1, q))
            pl.when(jnp.logical_and(t > 1, hi_s - 1 <= 7))(lambda: p_add(hi_s - 1, q))

        @pl.when(t == 2)
        def _():
            for zz in zpeer:
                f_2_in(zz).wait_recv()
            for cc in cpeer:
                f_3(cc).start()
            fa3[c] = fag[c]

    for q in range(4):
        pl.when(z == 7)(lambda: p_add(0, q))
        pl.when(z == 0)(lambda: p_add(7, q))

    def p_c(yy):
        return rc(pes.at[yy], per_.at[yy], pc_s.at[yy], pc_r.at[yy], z, other)

    def p_y(yy):
        return rc(ses.at[yy], ser.at[y], ps_s.at[yy], ps_r.at[y], z, 2 * yy + core)

    def p_y_in(yy):
        return rc(ses.at[yy], ser.at[yy], ps_s.at[yy], ps_r.at[yy], z, 2 * yy + core)

    for yy in ypeer + [y]:
        pes[yy] = enc(pb[2 * yy + 1 - core])
        p_c(yy).start()

    for yy in ypeer:
        p_c(yy).wait_recv()
        ses[yy] = enc(pb[2 * yy + core] + dec(per_[yy]))
        p_y(yy).start()
    p_c(y).wait_recv()
    new_a = pb[c] + dec(per_[y])
    for cc in cpeer:
        f_3_in(cc).wait_recv()
    new_a = new_a + fa3[...].reshape(C2, 128).astype(F32)
    for yy in ypeer:
        p_y_in(yy).wait_recv()
        new_a = new_a + dec(ser[yy])
    nag[c] = enc(new_a).reshape(8, 64, 128)

    def n_y(yy):
        return rc(nag.at[c], nag.at[c], ny_s.at[yy], ng_r.at[c], z, 2 * yy + core)

    def n_c(yy):
        piece = nag.at[2 * yy + core]
        return rc(piece, piece, nc_s.at[yy], ng_r.at[2 * yy + core], z, other)

    def n_in(j):
        return rc(nag.at[j], nag.at[j], nc_s.at[0], ng_r.at[j], z, other)

    for yy in ypeer:
        n_y(yy).start()
    n_c(y).start()

    def n_decode(j):
        lanes = pl.ds(pl.multiple_of(j * 128, 128), 128)
        hi, lo = split(dec(nag[j].reshape(C2, 128)))
        xh[:, lanes] = hi
        xl[:, lanes] = lo

    def t_z(zz):
        return rc(nag.at[zz, c], tz.at[z], tz_s.at[zz], tz_r.at[z], zz, c)

    def t_z_in(zz):
        return rc(nag.at[zz, c], tz.at[zz], tz_s.at[zz], tz_r.at[zz], zz, c)

    def t_n(r):
        return rc(tz.at[r], tn.at[c], tn_s.at[r], tn_r.at[c], z, r)

    def t_n_in(r):
        return rc(tz.at[r], tn.at[r], tn_s.at[r], tn_r.at[r], z, r)

    def n_take(j):
        pl.when(j != z)(lambda: t_z(j).start())
        n_decode(j)

    def f_add(yy, first=False):
        pair = pl.ds(pl.multiple_of(yy * 256, 256), 256)

        @pl.loop(0, 4)
        def _(i):
            lanes = pl.ds(pl.multiple_of(i * 256, 256), 256)
            c_hi = chi[pair, lanes]
            total = dot(xh[:, pair], c_hi) + dot(xl[:, pair], c_hi) + dot(xh[:, pair], clo[pair, lanes])
            total = total * FIELD_DOWN
            if first:
                fb[2 * i] = total[:, 0:128]
                fb[2 * i + 1] = total[:, 128:256]
            else:
                fb[2 * i] = fb[2 * i] + total[:, 0:128]
                fb[2 * i + 1] = fb[2 * i + 1] + total[:, 128:256]

    def n_near(yy):
        n_in(2 * yy + core).wait_recv()
        n_c(yy).start()
        n_take(2 * yy + core)

    def n_far(yy):
        n_in(2 * yy + 1 - core).wait_recv()
        n_take(2 * yy + 1 - core)

    n_take(c)
    n_far(y)
    f_add(y, True)
    n_near(ypeer[0])
    n_near(ypeer[1])
    n_far(ypeer[0])
    f_add(ypeer[0])
    n_near(ypeer[2])
    n_far(ypeer[1])
    f_add(ypeer[1])
    n_far(ypeer[2])
    tz[z] = nag[z, c]
    f_add(ypeer[2])

    def z_out(direction, dest, q, zz):
        rows = pl.ds(q * 128, 128)
        return rc(
            zs.at[direction, dest, rows], zr.at[direction, dest, rows],
            zr_s.at[direction, dest, q], zr_r.at[direction, dest, q], zz, c,
        )

    def z_step(direction, dest, first, last, zz):
        for q in range(4):
            rows = pl.ds(q * 128, 128)

            @pl.when(jnp.logical_and(first, jnp.logical_not(last)))
            def _():
                zs[direction, dest, rows] = enc(fb[dest, rows])

            @pl.when(jnp.logical_not(first))
            def _():
                z_out(direction, dest, q, zz).wait_recv()
                total = fb[dest, rows] + dec(zr[direction, dest, rows])

                @pl.when(last)
                def _():
                    fb[dest, rows] = total

                @pl.when(jnp.logical_not(last))
                def _():
                    zs[direction, dest, rows] = enc(total)

            @pl.when(jnp.logical_not(last))
            def _():
                z_out(direction, dest, q, zz).start()

    @pl.loop(0, 8)
    def _(t):
        @pl.when(t >= z)
        def _():
            z_step(0, 7 + z - t, z == 0, t == 7, up)

        @pl.when(t >= 7 - z)
        def _():
            z_step(1, t - 7 + z, z == 7, t == 7, down)

        @pl.when(t == 3)
        def _():
            for zz in zpeer:
                t_z_in(zz).wait_recv()
            for r in cpeer:
                t_n(r).start()
            tn[c] = tz[c]

        @pl.when(t == 6)
        def _():
            for r in cpeer:
                t_n_in(r).wait_recv()
            rows_a = dec(tn[...].reshape(C2, 128)).T
            hi, lo = split(rows_a)
            lo2 = (rows_a - hi.astype(F32) - lo.astype(F32)).astype(BF)
            back = (lax.broadcasted_iota(jnp.int32, shape_sq, 0) == source_column(lax.broadcasted_iota(jnp.int32, shape_sq, 1))).astype(F32).astype(BF)
            na_ref[...] = dot(hi, back, NT) + dot(lo, back, NT) + dot(lo2, back, NT)
            for k in range(2):
                hi_k = jnp.where(lane_k == k, hi.astype(F32), 0.0).astype(BF)
                lo_k = jnp.where(lane_k == k, lo.astype(F32), 0.0).astype(BF)
                fit = dot(hi_k, ball[...]) + dot(lo_k, ball[...])
                d2[k * 128:(k + 1) * 128, :] = (wk[k].astype(F32) - fit).astype(BF)

    field = fb[z] * (FIELD_UP * 8.0 / D)
    wide = jnp.concatenate([jnp.where(sub_k == 0, field, 0.0), jnp.where(sub_k == 1, field, 0.0)], axis=1)
    hi, lo = split(wide)
    xh[:, 0:256] = hi
    xl[:, 0:256] = lo

    def f_c(h):
        return rc(fcs.at[h], fcr.at[h], fc_s.at[h], fc_r.at[h], z, other)

    def f_y(h, yy):
        return rc(fys.at[h, yy], fyr.at[h, y], fy_s.at[h, yy], fy_r.at[h, y], z, 2 * yy + core)

    def f_y_in(h, yy):
        return rc(fys.at[h, yy], fyr.at[h, yy], fy_s.at[h, yy], fy_r.at[h, yy], z, 2 * yy + core)

    def f_z(h, zz):
        return rc(fzs.at[h, zz], fzr.at[h, z], fz_s.at[h, zz], fz_r.at[h, z], zz, c)

    def f_z_in(h, zz):
        return rc(fzs.at[h, zz], fzr.at[h, zz], fz_s.at[h, zz], fz_r.at[h, zz], zz, c)

    def half(which, h):
        rows = pl.ds(pl.multiple_of(which * 256, 256), 256)
        right = d2[:, h * 512:(h + 1) * 512]
        return (dot(xh[rows, 0:256], right) + dot(xl[rows, 0:256], right)).reshape(4, 64, 512)

    for h in range(2):
        fcs[h] = enc(half(1 - core, h))
        f_c(h).start()
    for h in range(2):
        p2[h] = half(core, h)
        f_c(h).wait_recv()
        for yy in ypeer:
            fys[h, yy] = enc(p2[h, yy] + dec(fcr[h, yy]))
            f_y(h, yy).start()
    for h in range(2):
        total = p2[h, y] + dec(fcr[h, y])
        for yy in ypeer:
            f_y_in(h, yy).wait_recv()
            total = total + dec(fyr[h, yy])
        fsum[h] = total.reshape(8, 8, 512)
        for zz in zpeer:
            mine = fsum[h, zz]
            fzs[h, zz] = enc(jnp.concatenate([mine[:, 0:256], mine[:, 256:512]], axis=0))
            f_z(h, zz).start()
    for h in range(2):
        rest = None
        for zz in zpeer:
            f_z_in(h, zz).wait_recv()
            got = dec(fzr[h, zz])
            rest = got if rest is None else rest + got
        gained = fsum[h, z] + jnp.concatenate([rest[0:8], rest[8:16]], axis=1)
        nb_ref[:, h * 512:(h + 1) * 512] = b_own[:, h * 512:(h + 1) * 512] + gained

    for zz in zpeer:
        b_z(zz).wait_send()
        f_2(zz).wait_send()
        t_z(zz).wait_send()
        for h in range(2):
            f_z(h, zz).wait_send()
        for yy in ypeer:
            b_y(yy, zz).wait_send()
    for r in cpeer:
        t_n(r).wait_send()
        f_1(r).wait_send()
        f_3(r).wait_send()
    for yy in ypeer:
        b_y(yy, z).wait_send()
        p_y(yy).wait_send()
        n_y(yy).wait_send()
        for h in range(2):
            f_y(h, yy).wait_send()
    for yy in ypeer + [y]:
        b_c(yy).wait_send()
        p_c(yy).wait_send()
        n_c(yy).wait_send()
    for h in range(2):
        f_c(h).wait_send()

    @pl.loop(0, 8)
    def _(s):
        for q in range(4):
            pl.when(jnp.logical_and(s <= z, z < 7))(lambda: x_out(0, s, q, up).wait_send())
            pl.when(jnp.logical_and(s >= z, z > 0))(lambda: x_out(1, s, q, down).wait_send())
            pl.when(s > z)(lambda: z_out(0, s, q, up).wait_send())
            pl.when(s < z)(lambda: z_out(1, s, q, down).wait_send())


def per_device(covariance, weight, factor_a, factor_b):
    n = weight.shape[0]
    vm = pl.BlockSpec(memory_space=pltpu.VMEM)
    blk = (8, C2, 128)
    dma = pltpu.SemaphoreType.DMA
    new_a, new_b = pl.pallas_call(
        kernel,
        name="refine",
        out_shape=(jax.ShapeDtypeStruct((n, C2), F32), jax.ShapeDtypeStruct((8, O), F32)),
        in_specs=[pl.BlockSpec(memory_space=pl.ANY), pl.BlockSpec(memory_space=pl.ANY), vm, vm],
        out_specs=(vm, vm),
        scratch_shapes=[
            pltpu.VMEM((1024, 1024), F32),
            pltpu.VMEM((n, 2, O), BF),
            pltpu.VMEM((2, n, O), BF),
            pltpu.VMEM((1024, 1024), BF),
            pltpu.VMEM((1024, 1024), BF),
            pltpu.VMEM((1024, 2048), BF),
            pltpu.VMEM((2, 4, 8, 16, 512), BF),
            pltpu.VMEM((C2, O), BF),
            pltpu.VMEM((128, C2), BF),
            pltpu.VMEM(blk, BF),
            pltpu.VMEM((C2, 1024), BF),
            pltpu.VMEM((C2, 1024), BF),
            pltpu.VMEM((8, 64, 128), BF),
            pltpu.VMEM((8, 64, 128), BF),
            pltpu.VMEM((8, 64, 128), BF),
            pltpu.VMEM((8, 64, 128), BF),
            pltpu.VMEM(blk, F32),
            pltpu.VMEM((4, C2, 128), BF),
            pltpu.VMEM((4, C2, 128), BF),
            pltpu.VMEM((4, C2, 128), BF),
            pltpu.VMEM((4, C2, 128), BF),
            pltpu.VMEM((8, 8, 64, 128), BF),
            pltpu.VMEM((8, 64, 128), BF),
            pltpu.VMEM((8, 64, 128), BF),
            pltpu.VMEM(blk, F32),
            pltpu.VMEM((2,) + blk, BF),
            pltpu.VMEM((2,) + blk, BF),
            pltpu.VMEM((256, O), BF),
            pltpu.VMEM((2, 4, 64, 512), F32),
            pltpu.VMEM((2, 4, 64, 512), BF),
            pltpu.VMEM((2, 4, 64, 512), BF),
            pltpu.VMEM((2, 4, 64, 512), BF),
            pltpu.VMEM((2, 4, 64, 512), BF),
            pltpu.VMEM((2, 8, 8, 512), F32),
            pltpu.VMEM((2, 8, 16, 256), BF),
            pltpu.VMEM((2, 8, 16, 256), BF),
            dma, dma,
            dma((8,)), dma((8,)), dma((4, 8)), dma((4, 8)), dma((4,)), dma((4,)),
            dma((8,)), dma((8,)), dma((8,)), dma((8,)), dma((8,)), dma((8,)),
            dma((2, 8, 4)), dma((8, 4)),
            dma((4,)), dma((4,)), dma((4,)), dma((4,)),
            dma((4,)), dma((4,)), dma((8,)),
            dma((8,)), dma((8,)), dma((8,)), dma((8,)),
            dma((2, 8, 4)), dma((2, 8, 4)),
            dma((2,)), dma((2,)), dma((2, 4)), dma((2, 4)), dma((2, 8)), dma((2, 8)),
        ],
        compiler_params=pltpu.CompilerParams(
            collective_id=0, has_side_effects=True, vmem_limit_bytes=56 * 2**20
        ),
    )(covariance, weight, factor_a, factor_b)
    return new_a.reshape(n, 2, R), new_b.reshape(2, 4, O)


def solution(mesh):
    in_specs = (
        P(("layer", "row"), "col"),
        P(("layer", "col", "row"), None, None),
        P(("layer", "col", "row"), None, None),
        P("layer", ("row", "col"), None),
    )
    out_specs = (P(("layer", "col", "row"), None, None), P("layer", ("row", "col"), None))
    return jax.shard_map(
        per_device, mesh=mesh, in_specs=in_specs, out_specs=out_specs, check_vma=False
    )
```

time: 141 us -> 129 us (0.915)
  Pallas kernels: 135 us -> 125 us
  local copies, waits for them, and re-layouts: 5.02 us -> 3.2 us
    pallas_call x1, Pallas kernels: 135 us -> 125 us  [per_device(): pl.pallas_call(kernel, name='refine', out_shape=(jax.ShapeDtypeStruct((n,...]
    unnamed x2 -> x0, local copies, waits for them, and re-layouts: 2.08 us -> none
    reshape x2, local copies, waits for them, and re-layouts: 1.49 us -> 3.2 us  [per_device(): return (new_a.reshape(n, 2, R), new_b.reshape(2, 4, O))]
where the time goes in v2:
time: 129 us
  Pallas kernels  125 us (97%)
  local copies, waits for them, and re-layouts  3.2 us (2%)
    pallas_call x1, Pallas kernels, per_device(): pl.pallas_call(kernel, name='refine', out_shape=(jax.ShapeDtypeStruct((n,...  125 us
    reshape x2, local copies, waits for them, and re-layouts, per_device(): return (new_a.reshape(n, 2, R), new_b.reshape(2, 4, O))  3.2 us

profile of v2, /device:TPU:1, one launch (start us, length us, event | category | flops | bytes accessed | tf_op | source)
XLA Modules:
  0.0 129.0 jit_solution(17527049732493372189)
XLA Ops:
  0.6 125.2 %refine.1 = (f32[128,512]{1,0:T(8,128)}, f32[8,1024]{1,0:T(8,128)}) custom-call(f32[1024,1024]{1,0:T(8,128)} %cov_hbm.1, bf16[128,2,1024]{2,1,0:T(2,128)(2,1)} %w_hbm.1, bf16[128,2,256]{2,1,0:T(2,128)(2,1)} %a_ref.1, bf16[2,4,1024]{2,1,0:T(4,128)(2,1)} %b_ref.1), custom_call_target="tpu_custom_call" | custom-call | tf_op jit(solution)/shard_map/refine/pallas_call | solution.py:543
  125.8 1.8 %reshape.10 = f32[128,2,256]{2,1,0:T(2,128)} reshape(f32[128,512]{1,0:T(8,128)} %get-tuple-element.4) | data formatting | bytes 524288 | tf_op jit(solution)/shard_map/reshape | solution.py:600
  127.6 1.4 %reshape.11 = f32[2,4,1024]{2,1,0:T(4,128)} reshape(f32[8,1024]{1,0:T(8,128)} %get-tuple-element.5) | data formatting | bytes 65536 | tf_op jit(solution)/shard_map/reshape | solution.py:600

commit v3 on v2

--- a/solution.py
+++ b/solution.py
@@ -53,9 +53,9 @@
 def kernel(
     cov_hbm, w_hbm, a_ref, b_ref, na_ref, nb_ref,
     cov, wv, wk, chi, clo, ccat, gat, ball, aint, xg, xh, xl, fas, fa1, fag, fa3, pb, pes, per_, ses, ser,
-    nag, tz, tn, fb, zs, zr, d2, p2, fcs, fcr, fys, fyr, fsum, fzs, fzr,
+    nag, tz, tn, fb, zms, zmr, zs, zr, d2, p2, fcs, fcr, fys, fyr, fsum, fzs, fzr,
     cov_sem, w_sem, bz_s, bz_r, by_s, by_r, bc_s, bc_r, f1_s, f1_r, f2_s, f2_r, f3_s, f3_r, xg_s, xg_r,
-    pc_s, pc_r, ps_s, ps_r, ny_s, nc_s, ng_r, tz_s, tz_r, tn_s, tn_r, zr_s, zr_r,
+    pc_s, pc_r, ps_s, ps_r, ny_s, nc_s, ng_r, tz_s, tz_r, tn_s, tn_r, zm_s, zm_r, zr_s, zr_r,
     fc_s, fc_r, fy_s, fy_r, fz_s, fz_r,
 ):
     layer = lax.axis_index("layer")
@@ -64,6 +64,10 @@
     y = lax.div(c, 2)
     core = lax.rem(c, 2)
     other = c + 1 - 2 * core
+    m = lax.div(z, 2)
+    par = lax.rem(z, 2)
+    mate = z + 1 - 2 * par
+    up, down = lax.rem(z + 2, 8), lax.rem(z + 6, 8)
 
     def rc(src, dst, ss, rs, zz, cc):
         return pltpu.make_async_remote_copy(
@@ -152,10 +156,24 @@
         for yy in ypeer:
             b_y(yy, zz).start()
 
+    def cov_split(i):
+        rows = pl.ds(pl.multiple_of(i * 128, 128), 128)
+        hi, lo = split(cov[rows, :])
+        chi[rows, :] = hi
+        clo[rows, :] = lo
+        for s in range(8):
+            ccat[rows, s * 256:s * 256 + 128] = hi[:, s * 128:(s + 1) * 128]
+            ccat[rows, s * 256 + 128:(s + 1) * 256] = lo[:, s * 128:(s + 1) * 128]
+        pb[i] = jnp.zeros((C2, 128), F32)
+
+    cov_copy.wait()
+    cov_split(0)
+
     @pl.loop(1, 8)
     def _(t):
         pl.when(z - t >= 0)(lambda: b_forward(z - t))
         pl.when(z + t <= 7)(lambda: b_forward(z + t))
+        cov_split(t)
 
     b_c(y).start()
 
@@ -210,122 +228,146 @@
         piece = xg.at[s, pl.ds(q * 128, 128)]
         return rc(piece, piece, xg_s.at[direction, s, q], xg_r.at[s, q], zz, c)
 
-    up, down = lax.rem(z + 1, 8), lax.rem(z + 7, 8)
-    for q in range(4):
-        pl.when(z < 7)(lambda: x_out(0, z, q, up).start())
-        pl.when(z > 0)(lambda: x_out(1, z, q, down).start())
-
-    def x_decode(s, q):
-        rows = pl.ds(q * 128, 128)
+    def x_pass(s, q, more_up, more_down):
+        pl.when(more_up)(lambda: x_out(0, s, q, up).start())
+        pl.when(more_down)(lambda: x_out(1, s, q, down).start())
+        x_out(2, s, q, mate).start()
+
+    def x_decode(s, h):
+        rows = pl.ds(h * 256, 256)
         lanes = pl.ds(pl.multiple_of(s * 128, 128), 128)
         hi, lo = split(dec(xg[s, rows]))
         xh[rows, lanes] = hi
         xl[rows, lanes] = lo
 
-    def p_add(s, q):
+    def p_add(s, h):
+        rows = pl.ds(h * 256, 256)
         lanes = pl.ds(pl.multiple_of(s * 128, 128), 128)
         wide = pl.ds(pl.multiple_of(s * 256, 256), 256)
-        hi = xh[:, lanes]
-        c_hi = chi[q * 256:(q + 1) * 256, lanes]
-        c_both = ccat[q * 256:(q + 1) * 256, wide]
-        total = dot(jnp.concatenate([hi, hi], axis=1), c_both, NT) + dot(xl[:, lanes], c_hi, NT)
-        total = total * (4.0 / O)
-        pb[2 * q] = pb[2 * q] + total[:, 0:128]
-        pb[2 * q + 1] = pb[2 * q + 1] + total[:, 128:256]
-
-    cov_copy.wait()
-
-    @pl.loop(0, 8)
-    def _(i):
-        rows = pl.ds(pl.multiple_of(i * 128, 128), 128)
-        hi, lo = split(cov[rows, :])
-        chi[rows, :] = hi
-        clo[rows, :] = lo
-        for s in range(8):
-            ccat[rows, s * 256:s * 256 + 128] = hi[:, s * 128:(s + 1) * 128]
-            ccat[rows, s * 256 + 128:(s + 1) * 256] = lo[:, s * 128:(s + 1) * 128]
-        pb[i] = jnp.zeros((C2, 128), F32)
-
-    for q in range(4):
-        x_decode(z, q)
-
-    @pl.loop(1, 8)
-    def _(t):
-        lo_s, hi_s = z - t, z + t
-        for q in range(4):
-            @pl.when(lo_s >= 0)
-            def _():
-                x_out(0, lo_s, q, up).wait_recv()
-                pl.when(z < 7)(lambda: x_out(0, lo_s, q, up).start())
-
-            @pl.when(hi_s <= 7)
-            def _():
-                x_out(1, hi_s, q, down).wait_recv()
-                pl.when(z > 0)(lambda: x_out(1, hi_s, q, down).start())
-
-            pl.when(lo_s >= 0)(lambda: x_decode(lo_s, q))
-            pl.when(hi_s <= 7)(lambda: x_decode(hi_s, q))
-            pl.when(lo_s + 1 >= 0)(lambda: p_add(lo_s + 1, q))
-            pl.when(jnp.logical_and(t > 1, hi_s - 1 <= 7))(lambda: p_add(hi_s - 1, q))
-
-        @pl.when(t == 2)
-        def _():
-            for zz in zpeer:
-                f_2_in(zz).wait_recv()
+
+        @pl.loop(0, 4)
+        def _(i):
+            part = pl.ds(pl.multiple_of(i * 256, 256), 256)
+            hi = xh[rows, lanes]
+            both = jnp.concatenate([hi, hi], axis=1)
+            total = dot(both, ccat[part, wide], NT) + dot(xl[rows, lanes], chi[part, lanes], NT)
+            total = total * (4.0 / O)
+            pb[2 * i, rows] = pb[2 * i, rows] + total[:, 0:128]
+            pb[2 * i + 1, rows] = pb[2 * i + 1, rows] + total[:, 128:256]
+
+    def x_use(s, h):
+        x_decode(s, h)
+        p_add(s, h)
+
+    def x_mate(u, h):
+        def take(s):
+            for q in (2 * h, 2 * h + 1):
+                x_out(2, s, q, mate).wait_recv()
+            x_use(s, h)
+
+        if u == 0:
+            take(mate)
+        else:
+            pl.when(m - u >= 0)(lambda: take(2 * (m - u) + 1 - par))
+            pl.when(m + u <= 3)(lambda: take(2 * (m + u) + 1 - par))
+
+    def x_step(u, h):
+        pair = (2 * h, 2 * h + 1)
+        if u == 0:
+            for q in pair:
+                x_pass(z, q, m < 3, m > 0)
+            x_use(z, h)
+            return
+        low, high = 2 * (m - u) + par, 2 * (m + u) + par
+
+        def come(s, going_up):
+            for q in pair:
+                x_out(0, s, q, up).wait_recv()
+                x_pass(s, q, jnp.logical_and(going_up, m < 3), jnp.logical_and(jnp.logical_not(going_up), m > 0))
+
+        pl.when(m - u >= 0)(lambda: come(low, True))
+        pl.when(m + u <= 3)(lambda: come(high, False))
+        pl.when(m - u >= 0)(lambda: x_use(low, h))
+        pl.when(m + u <= 3)(lambda: x_use(high, h))
+        x_mate(u - 1, h)
+
+    def left_factors():
+        for zz in zpeer:
+            f_2_in(zz).wait_recv()
+        for cc in cpeer:
+            f_3(cc).start()
+        fa3[c] = fag[c]
+
+    def cols(h):
+        return pl.ds(h * 256, 256)
+
+    def p_c(h, yy):
+        return rc(pes.at[yy, cols(h)], per_.at[yy, cols(h)], pc_s.at[h, yy], pc_r.at[h, yy], z, other)
+
+    def p_y(h, yy):
+        return rc(ses.at[yy, cols(h)], ser.at[y, cols(h)], ps_s.at[h, yy], ps_r.at[h, y], z, 2 * yy + core)
+
+    def p_y_in(h, yy):
+        return rc(ses.at[yy, cols(h)], ser.at[yy, cols(h)], ps_s.at[h, yy], ps_r.at[h, yy], z, 2 * yy + core)
+
+    def p_core(h):
+        for yy in ypeer + [y]:
+            pes[yy, cols(h)] = enc(pb[2 * yy + 1 - core, cols(h)])
+            p_c(h, yy).start()
+
+    def p_plane(h):
+        for yy in ypeer:
+            p_c(h, yy).wait_recv()
+            ses[yy, cols(h)] = enc(pb[2 * yy + core, cols(h)] + dec(per_[yy, cols(h)]))
+            p_y(h, yy).start()
+
+    def eighths(h):
+        return pl.ds(4 * h, 4)
+
+    def n_y(h, yy):
+        piece = nag.at[c, eighths(h)]
+        return rc(piece, piece, ny_s.at[h, yy], ng_r.at[h, c], z, 2 * yy + core)
+
+    def n_c(h, yy):
+        piece = nag.at[2 * yy + core, eighths(h)]
+        return rc(piece, piece, nc_s.at[h, yy], ng_r.at[h, 2 * yy + core], z, other)
+
+    def n_in(h, j):
+        piece = nag.at[j, eighths(h)]
+        return rc(piece, piece, nc_s.at[h, 0], ng_r.at[h, j], z, other)
+
+    def p_end(h):
+        p_c(h, y).wait_recv()
+        new_a = pb[c, cols(h)] + dec(per_[y, cols(h)])
+        for yy in ypeer:
+            p_y_in(h, yy).wait_recv()
+            new_a = new_a + dec(ser[yy, cols(h)])
+        if h == 0:
             for cc in cpeer:
-                f_3(cc).start()
-            fa3[c] = fag[c]
-
-    for q in range(4):
-        pl.when(z == 7)(lambda: p_add(0, q))
-        pl.when(z == 0)(lambda: p_add(7, q))
-
-    def p_c(yy):
-        return rc(pes.at[yy], per_.at[yy], pc_s.at[yy], pc_r.at[yy], z, other)
-
-    def p_y(yy):
-        return rc(ses.at[yy], ser.at[y], ps_s.at[yy], ps_r.at[y], z, 2 * yy + core)
-
-    def p_y_in(yy):
-        return rc(ses.at[yy], ser.at[yy], ps_s.at[yy], ps_r.at[yy], z, 2 * yy + core)
-
-    for yy in ypeer + [y]:
-        pes[yy] = enc(pb[2 * yy + 1 - core])
-        p_c(yy).start()
-
-    for yy in ypeer:
-        p_c(yy).wait_recv()
-        ses[yy] = enc(pb[2 * yy + core] + dec(per_[yy]))
-        p_y(yy).start()
-    p_c(y).wait_recv()
-    new_a = pb[c] + dec(per_[y])
-    for cc in cpeer:
-        f_3_in(cc).wait_recv()
-    new_a = new_a + fa3[...].reshape(C2, 128).astype(F32)
-    for yy in ypeer:
-        p_y_in(yy).wait_recv()
-        new_a = new_a + dec(ser[yy])
-    nag[c] = enc(new_a).reshape(8, 64, 128)
-
-    def n_y(yy):
-        return rc(nag.at[c], nag.at[c], ny_s.at[yy], ng_r.at[c], z, 2 * yy + core)
-
-    def n_c(yy):
-        piece = nag.at[2 * yy + core]
-        return rc(piece, piece, nc_s.at[yy], ng_r.at[2 * yy + core], z, other)
-
-    def n_in(j):
-        return rc(nag.at[j], nag.at[j], nc_s.at[0], ng_r.at[j], z, other)
-
-    for yy in ypeer:
-        n_y(yy).start()
-    n_c(y).start()
-
-    def n_decode(j):
-        lanes = pl.ds(pl.multiple_of(j * 128, 128), 128)
-        hi, lo = split(dec(nag[j].reshape(C2, 128)))
-        xh[:, lanes] = hi
-        xl[:, lanes] = lo
+                f_3_in(cc).wait_recv()
+        new_a = new_a + fa3[eighths(h)].reshape(256, 128).astype(F32)
+        nag[c, eighths(h)] = enc(new_a).reshape(4, 64, 128)
+        for yy in ypeer:
+            n_y(h, yy).start()
+        n_c(h, y).start()
+
+    x_step(0, 0)
+    x_step(1, 0)
+    x_step(0, 1)
+    x_step(2, 0)
+    x_step(1, 1)
+    x_step(3, 0)
+    left_factors()
+    x_step(2, 1)
+    x_mate(3, 0)
+    p_core(0)
+    x_step(3, 1)
+    p_plane(0)
+    x_mate(3, 1)
+    p_core(1)
+    p_plane(1)
+    p_end(0)
+    p_end(1)
 
     def t_z(zz):
         return rc(nag.at[zz, c], tz.at[z], tz_s.at[zz], tz_r.at[z], zz, c)
@@ -339,113 +381,139 @@
     def t_n_in(r):
         return rc(tz.at[r], tn.at[r], tn_s.at[r], tn_r.at[r], z, r)
 
-    def n_take(j):
-        pl.when(j != z)(lambda: t_z(j).start())
-        n_decode(j)
-
-    def f_add(yy, first=False):
+    def n_take(j, h):
+        if h == 1:
+            pl.when(j != z)(lambda: t_z(j).start())
+        lanes = pl.ds(pl.multiple_of(j * 128, 128), 128)
+        hi, lo = split(dec(nag[j, eighths(h)].reshape(256, 128)))
+        xh[cols(h), lanes] = hi
+        xl[cols(h), lanes] = lo
+
+    def f_add(yy, h, first=False):
         pair = pl.ds(pl.multiple_of(yy * 256, 256), 256)
+        rows = cols(h)
 
         @pl.loop(0, 4)
         def _(i):
             lanes = pl.ds(pl.multiple_of(i * 256, 256), 256)
             c_hi = chi[pair, lanes]
-            total = dot(xh[:, pair], c_hi) + dot(xl[:, pair], c_hi) + dot(xh[:, pair], clo[pair, lanes])
+            total = dot(xh[rows, pair], c_hi) + dot(xl[rows, pair], c_hi) + dot(xh[rows, pair], clo[pair, lanes])
             total = total * FIELD_DOWN
             if first:
-                fb[2 * i] = total[:, 0:128]
-                fb[2 * i + 1] = total[:, 128:256]
+                fb[2 * i, rows] = total[:, 0:128]
+                fb[2 * i + 1, rows] = total[:, 128:256]
             else:
-                fb[2 * i] = fb[2 * i] + total[:, 0:128]
-                fb[2 * i + 1] = fb[2 * i + 1] + total[:, 128:256]
-
-    def n_near(yy):
-        n_in(2 * yy + core).wait_recv()
-        n_c(yy).start()
-        n_take(2 * yy + core)
-
-    def n_far(yy):
-        n_in(2 * yy + 1 - core).wait_recv()
-        n_take(2 * yy + 1 - core)
-
-    n_take(c)
-    n_far(y)
-    f_add(y, True)
-    n_near(ypeer[0])
-    n_near(ypeer[1])
-    n_far(ypeer[0])
-    f_add(ypeer[0])
-    n_near(ypeer[2])
-    n_far(ypeer[1])
-    f_add(ypeer[1])
-    n_far(ypeer[2])
-    tz[z] = nag[z, c]
-    f_add(ypeer[2])
-
-    def z_out(direction, dest, q, zz):
+                fb[2 * i, rows] = fb[2 * i, rows] + total[:, 0:128]
+                fb[2 * i + 1, rows] = fb[2 * i + 1, rows] + total[:, 128:256]
+
+    def n_near(yy, h):
+        n_in(h, 2 * yy + core).wait_recv()
+        n_c(h, yy).start()
+        n_take(2 * yy + core, h)
+
+    def n_far(yy, h):
+        n_in(h, 2 * yy + 1 - core).wait_recv()
+        n_take(2 * yy + 1 - core, h)
+
+    def second(h):
+        n_take(c, h)
+        n_far(y, h)
+        f_add(y, h, True)
+        n_near(ypeer[0], h)
+        n_near(ypeer[1], h)
+        n_far(ypeer[0], h)
+        f_add(ypeer[0], h)
+        n_near(ypeer[2], h)
+        n_far(ypeer[1], h)
+        f_add(ypeer[1], h)
+        n_far(ypeer[2], h)
+        f_add(ypeer[2], h)
+
+    def z_mate(d, q):
+        rows = pl.ds(q * 128, 128)
+        return rc(zms.at[d, rows], zmr.at[d, rows], zm_s.at[d, q], zm_r.at[d, q], mate, c)
+
+    def z_out(direction, d, q, zz):
         rows = pl.ds(q * 128, 128)
         return rc(
-            zs.at[direction, dest, rows], zr.at[direction, dest, rows],
-            zr_s.at[direction, dest, q], zr_r.at[direction, dest, q], zz, c,
+            zs.at[direction, d, rows], zr.at[direction, d, rows],
+            zr_s.at[direction, d, q], zr_r.at[direction, d, q], zz, c,
         )
 
-    def z_step(direction, dest, first, last, zz):
-        for q in range(4):
+    def z_start(h):
+        for k in range(4):
+            d = 2 * lax.select(m < 2, 3 - k, k) + 1 - par
+            for q in (2 * h, 2 * h + 1):
+                rows = pl.ds(q * 128, 128)
+                zms[d, rows] = enc(fb[d, rows])
+                z_mate(d, q).start()
+
+    def z_pass(direction, d, h, first, zz):
+        for q in (2 * h, 2 * h + 1):
             rows = pl.ds(q * 128, 128)
-
-            @pl.when(jnp.logical_and(first, jnp.logical_not(last)))
+            z_mate(d, q).wait_recv()
+
+            @pl.when(first)
             def _():
-                zs[direction, dest, rows] = enc(fb[dest, rows])
+                zs[direction, d, rows] = enc(fb[d, rows] + dec(zmr[d, rows]))
 
             @pl.when(jnp.logical_not(first))
             def _():
-                z_out(direction, dest, q, zz).wait_recv()
-                total = fb[dest, rows] + dec(zr[direction, dest, rows])
-
-                @pl.when(last)
-                def _():
-                    fb[dest, rows] = total
-
-                @pl.when(jnp.logical_not(last))
-                def _():
-                    zs[direction, dest, rows] = enc(total)
-
-            @pl.when(jnp.logical_not(last))
+                z_out(direction, d, q, zz).wait_recv()
+                zs[direction, d, rows] = enc(fb[d, rows] + dec(zmr[d, rows]) + dec(zr[direction, d, rows]))
+
+            z_out(direction, d, q, zz).start()
+
+    def z_step(t, h):
+        pl.when(t >= m)(lambda: z_pass(0, 2 * (3 + m - t) + par, h, m == 0, up))
+        pl.when(t >= 3 - m)(lambda: z_pass(1, 2 * (t - 3 + m) + par, h, m == 3, down))
+
+    def z_end(h):
+        for q in (2 * h, 2 * h + 1):
+            rows = pl.ds(q * 128, 128)
+            z_mate(z, q).wait_recv()
+            fb[z, rows] = fb[z, rows] + dec(zmr[z, rows])
+
+            @pl.when(m > 0)
             def _():
-                z_out(direction, dest, q, zz).start()
-
-    @pl.loop(0, 8)
-    def _(t):
-        @pl.when(t >= z)
-        def _():
-            z_step(0, 7 + z - t, z == 0, t == 7, up)
-
-        @pl.when(t >= 7 - z)
-        def _():
-            z_step(1, t - 7 + z, z == 7, t == 7, down)
-
-        @pl.when(t == 3)
-        def _():
-            for zz in zpeer:
-                t_z_in(zz).wait_recv()
-            for r in cpeer:
-                t_n(r).start()
-            tn[c] = tz[c]
-
-        @pl.when(t == 6)
-        def _():
-            for r in cpeer:
-                t_n_in(r).wait_recv()
-            rows_a = dec(tn[...].reshape(C2, 128)).T
-            hi, lo = split(rows_a)
-            lo2 = (rows_a - hi.astype(F32) - lo.astype(F32)).astype(BF)
-            back = (lax.broadcasted_iota(jnp.int32, shape_sq, 0) == source_column(lax.broadcasted_iota(jnp.int32, shape_sq, 1))).astype(F32).astype(BF)
-            na_ref[...] = dot(hi, back, NT) + dot(lo, back, NT) + dot(lo2, back, NT)
-            for k in range(2):
-                hi_k = jnp.where(lane_k == k, hi.astype(F32), 0.0).astype(BF)
-                lo_k = jnp.where(lane_k == k, lo.astype(F32), 0.0).astype(BF)
-                fit = dot(hi_k, ball[...]) + dot(lo_k, ball[...])
-                d2[k * 128:(k + 1) * 128, :] = (wk[k].astype(F32) - fit).astype(BF)
+                z_out(0, z, q, up).wait_recv()
+                fb[z, rows] = fb[z, rows] + dec(zr[0, z, rows])
+
+            @pl.when(m < 3)
+            def _():
+                z_out(1, z, q, down).wait_recv()
+                fb[z, rows] = fb[z, rows] + dec(zr[1, z, rows])
+
+    second(0)
+    z_start(0)
+    second(1)
+    tz[z] = nag[z, c]
+    z_start(1)
+    z_step(0, 0)
+    z_step(1, 0)
+    z_step(0, 1)
+    z_step(2, 0)
+    z_step(1, 1)
+    for zz in zpeer:
+        t_z_in(zz).wait_recv()
+    for r in cpeer:
+        t_n(r).start()
+    tn[c] = tz[c]
+    z_end(0)
+    z_step(2, 1)
+    for r in cpeer:
+        t_n_in(r).wait_recv()
+    rows_a = dec(tn[...].reshape(C2, 128)).T
+    hi, lo = split(rows_a)
+    lo2 = (rows_a - hi.astype(F32) - lo.astype(F32)).astype(BF)
+    back = (lax.broadcasted_iota(jnp.int32, shape_sq, 0) == source_column(lax.broadcasted_iota(jnp.int32, shape_sq, 1))).astype(F32).astype(BF)
+    na_ref[...] = dot(hi, back, NT) + dot(lo, back, NT) + dot(lo2, back, NT)
+    for k in range(2):
+        hi_k = jnp.where(lane_k == k, hi.astype(F32), 0.0).astype(BF)
+        lo_k = jnp.where(lane_k == k, lo.astype(F32), 0.0).astype(BF)
+        fit = dot(hi_k, ball[...]) + dot(lo_k, ball[...])
+        d2[k * 128:(k + 1) * 128, :] = (wk[k].astype(F32) - fit).astype(BF)
+    z_end(1)
 
     field = fb[z] * (FIELD_UP * 8.0 / D)
     wide = jnp.concatenate([jnp.where(sub_k == 0, field, 0.0), jnp.where(sub_k == 1, field, 0.0)], axis=1)
@@ -515,24 +583,28 @@
         f_3(r).wait_send()
     for yy in ypeer:
         b_y(yy, z).wait_send()
-        p_y(yy).wait_send()
-        n_y(yy).wait_send()
         for h in range(2):
+            p_y(h, yy).wait_send()
+            n_y(h, yy).wait_send()
             f_y(h, yy).wait_send()
     for yy in ypeer + [y]:
         b_c(yy).wait_send()
-        p_c(yy).wait_send()
-        n_c(yy).wait_send()
+        for h in range(2):
+            p_c(h, yy).wait_send()
+            n_c(h, yy).wait_send()
     for h in range(2):
         f_c(h).wait_send()
 
-    @pl.loop(0, 8)
-    def _(s):
+    @pl.loop(0, 4)
+    def _(e):
+        s = 2 * e + par
         for q in range(4):
-            pl.when(jnp.logical_and(s <= z, z < 7))(lambda: x_out(0, s, q, up).wait_send())
-            pl.when(jnp.logical_and(s >= z, z > 0))(lambda: x_out(1, s, q, down).wait_send())
-            pl.when(s > z)(lambda: z_out(0, s, q, up).wait_send())
-            pl.when(s < z)(lambda: z_out(1, s, q, down).wait_send())
+            pl.when(jnp.logical_and(e <= m, m < 3))(lambda: x_out(0, s, q, up).wait_send())
+            pl.when(jnp.logical_and(e >= m, m > 0))(lambda: x_out(1, s, q, down).wait_send())
+            x_out(2, s, q, mate).wait_send()
+            z_mate(2 * e + 1 - par, q).wait_send()
+            pl.when(e > m)(lambda: z_out(0, s, q, up).wait_send())
+            pl.when(e < m)(lambda: z_out(1, s, q, down).wait_send())
 
 
 def per_device(covariance, weight, factor_a, factor_b):
@@ -572,6 +644,8 @@
             pltpu.VMEM((8, 64, 128), BF),
             pltpu.VMEM((8, 64, 128), BF),
             pltpu.VMEM(blk, F32),
+            pltpu.VMEM(blk, BF),
+            pltpu.VMEM(blk, BF),
             pltpu.VMEM((2,) + blk, BF),
             pltpu.VMEM((2,) + blk, BF),
             pltpu.VMEM((256, O), BF),
@@ -586,15 +660,15 @@
             dma, dma,
             dma((8,)), dma((8,)), dma((4, 8)), dma((4, 8)), dma((4,)), dma((4,)),
             dma((8,)), dma((8,)), dma((8,)), dma((8,)), dma((8,)), dma((8,)),
-            dma((2, 8, 4)), dma((8, 4)),
-            dma((4,)), dma((4,)), dma((4,)), dma((4,)),
-            dma((4,)), dma((4,)), dma((8,)),
+            dma((3, 8, 4)), dma((8, 4)),
+            dma((2, 4)), dma((2, 4)), dma((2, 4)), dma((2, 4)),
+            dma((2, 4)), dma((2, 4)), dma((2, 8)),
             dma((8,)), dma((8,)), dma((8,)), dma((8,)),
-            dma((2, 8, 4)), dma((2, 8, 4)),
+            dma((8, 4)), dma((8, 4)), dma((2, 8, 4)), dma((2, 8, 4)),
             dma((2,)), dma((2,)), dma((2, 4)), dma((2, 4)), dma((2, 8)), dma((2, 8)),
         ],
         compiler_params=pltpu.CompilerParams(
-            collective_id=0, has_side_effects=True, vmem_limit_bytes=56 * 2**20
+            collective_id=0, has_side_effects=True, vmem_limit_bytes=52 * 2**20
         ),
     )(covariance, weight, factor_a, factor_b)
     return new_a.reshape(n, 2, R), new_b.reshape(2, 4, O)

time: 129 us -> 136 us (1.054)
  Pallas kernels: 125 us -> 131 us
    pallas_call x1, Pallas kernels: 125 us -> 131 us  [per_device(): pl.pallas_call(kernel, name='refine', out_shape=(jax.ShapeDtypeStruct((n,...]
    unnamed x0 -> x6, local copies, waits for them, and re-layouts: none -> 2.66 us
    reshape x2, local copies, waits for them, and re-layouts: 3.2 us -> 1.49 us  [per_device(): return (new_a.reshape(n, 2, R), new_b.reshape(2, 4, O))]
where the time goes in v3:
time: 136 us
  Pallas kernels  131 us (96%)
  local copies, waits for them, and re-layouts  4.15 us (3%)
    pallas_call x1, Pallas kernels, per_device(): pl.pallas_call(kernel, name='refine', out_shape=(jax.ShapeDtypeStruct((n,...  131 us

profile of v3, /device:TPU:1, one launch (start us, length us, event | category | flops | bytes accessed | tf_op | source)
XLA Modules:
  0.0 135.6 jit_solution(2004831710874681906)
XLA Ops:
  0.6 0.0 copy-start
  0.6 1.0 copy-done
  1.7 0.0 copy-start.1
  1.7 0.9 copy-done.1
  2.6 0.0 copy-start.2
  2.6 0.7 copy-done.2
  3.3 130.8 %refine.1 = (f32[128,512]{1,0:T(8,128)S(1)}, f32[8,1024]{1,0:T(8,128)S(1)}) custom-call(f32[1024,1024]{1,0:T(8,128)} %cov_hbm.1, bf16[128,2,1024]{2,1,0:T(2,128)(2,1)S(1)} %copy-done, bf16[128,2,256]{2,1,0:T(2,128)(2,1)S(1)} %copy-done.1, bf16[2,4,1024]{2,1,0:T(4,128)(2,1)S(1)} %copy-done.2), custom_call_target="tpu_custom_call" | custom-call | tf_op jit(solution)/shard_map/refine/pallas_call | solution.py:615
  134.1 0.9 reshape.10
  134.9 0.6 reshape.11
Async XLA Ops:
  0.6 1.0 copy-start
  1.7 0.9 copy-start.1
  2.6 0.7 copy-start.2

commit v4 on v3

--- a/solution.py
+++ b/solution.py
@@ -53,9 +53,9 @@
 def kernel(
     cov_hbm, w_hbm, a_ref, b_ref, na_ref, nb_ref,
     cov, wv, wk, chi, clo, ccat, gat, ball, aint, xg, xh, xl, fas, fa1, fag, fa3, pb, pes, per_, ses, ser,
-    nag, tz, tn, fb, zms, zmr, zs, zr, d2, p2, fcs, fcr, fys, fyr, fsum, fzs, fzr,
+    nag, tz, tn, fb, zs, zr, d2, p2, fcs, fcr, fys, fyr, fsum, fzs, fzr,
     cov_sem, w_sem, bz_s, bz_r, by_s, by_r, bc_s, bc_r, f1_s, f1_r, f2_s, f2_r, f3_s, f3_r, xg_s, xg_r,
-    pc_s, pc_r, ps_s, ps_r, ny_s, nc_s, ng_r, tz_s, tz_r, tn_s, tn_r, zm_s, zm_r, zr_s, zr_r,
+    pc_s, pc_r, ps_s, ps_r, ny_s, nc_s, ng_r, tz_s, tz_r, tn_s, tn_r, zr_s, zr_r,
     fc_s, fc_r, fy_s, fy_r, fz_s, fz_r,
 ):
     layer = lax.axis_index("layer")
@@ -64,10 +64,7 @@
     y = lax.div(c, 2)
     core = lax.rem(c, 2)
     other = c + 1 - 2 * core
-    m = lax.div(z, 2)
-    par = lax.rem(z, 2)
-    mate = z + 1 - 2 * par
-    up, down = lax.rem(z + 2, 8), lax.rem(z + 6, 8)
+    up, down = lax.rem(z + 1, 8), lax.rem(z + 7, 8)
 
     def rc(src, dst, ss, rs, zz, cc):
         return pltpu.make_async_remote_copy(
@@ -228,75 +225,61 @@
         piece = xg.at[s, pl.ds(q * 128, 128)]
         return rc(piece, piece, xg_s.at[direction, s, q], xg_r.at[s, q], zz, c)
 
-    def x_pass(s, q, more_up, more_down):
-        pl.when(more_up)(lambda: x_out(0, s, q, up).start())
-        pl.when(more_down)(lambda: x_out(1, s, q, down).start())
-        x_out(2, s, q, mate).start()
-
-    def x_decode(s, h):
-        rows = pl.ds(h * 256, 256)
+    for q in range(4):
+        pl.when(z < 7)(lambda: x_out(0, z, q, up).start())
+        pl.when(z > 0)(lambda: x_out(1, z, q, down).start())
+
+    def x_decode(s, q):
+        rows = pl.ds(q * 128, 128)
         lanes = pl.ds(pl.multiple_of(s * 128, 128), 128)
         hi, lo = split(dec(xg[s, rows]))
         xh[rows, lanes] = hi
         xl[rows, lanes] = lo
 
-    def p_add(s, h):
-        rows = pl.ds(h * 256, 256)
+    def p_add(s, q):
         lanes = pl.ds(pl.multiple_of(s * 128, 128), 128)
         wide = pl.ds(pl.multiple_of(s * 256, 256), 256)
-
-        @pl.loop(0, 4)
-        def _(i):
-            part = pl.ds(pl.multiple_of(i * 256, 256), 256)
-            hi = xh[rows, lanes]
-            both = jnp.concatenate([hi, hi], axis=1)
-            total = dot(both, ccat[part, wide], NT) + dot(xl[rows, lanes], chi[part, lanes], NT)
-            total = total * (4.0 / O)
-            pb[2 * i, rows] = pb[2 * i, rows] + total[:, 0:128]
-            pb[2 * i + 1, rows] = pb[2 * i + 1, rows] + total[:, 128:256]
-
-    def x_use(s, h):
-        x_decode(s, h)
-        p_add(s, h)
-
-    def x_mate(u, h):
-        def take(s):
-            for q in (2 * h, 2 * h + 1):
-                x_out(2, s, q, mate).wait_recv()
-            x_use(s, h)
-
-        if u == 0:
-            take(mate)
-        else:
-            pl.when(m - u >= 0)(lambda: take(2 * (m - u) + 1 - par))
-            pl.when(m + u <= 3)(lambda: take(2 * (m + u) + 1 - par))
-
-    def x_step(u, h):
-        pair = (2 * h, 2 * h + 1)
-        if u == 0:
-            for q in pair:
-                x_pass(z, q, m < 3, m > 0)
-            x_use(z, h)
-            return
-        low, high = 2 * (m - u) + par, 2 * (m + u) + par
-
-        def come(s, going_up):
-            for q in pair:
-                x_out(0, s, q, up).wait_recv()
-                x_pass(s, q, jnp.logical_and(going_up, m < 3), jnp.logical_and(jnp.logical_not(going_up), m > 0))
-
-        pl.when(m - u >= 0)(lambda: come(low, True))
-        pl.when(m + u <= 3)(lambda: come(high, False))
-        pl.when(m - u >= 0)(lambda: x_use(low, h))
-        pl.when(m + u <= 3)(lambda: x_use(high, h))
-        x_mate(u - 1, h)
-
-    def left_factors():
-        for zz in zpeer:
-            f_2_in(zz).wait_recv()
-        for cc in cpeer:
-            f_3(cc).start()
-        fa3[c] = fag[c]
+        hi = xh[:, lanes]
+        c_hi = chi[q * 256:(q + 1) * 256, lanes]
+        c_both = ccat[q * 256:(q + 1) * 256, wide]
+        total = dot(jnp.concatenate([hi, hi], axis=1), c_both, NT) + dot(xl[:, lanes], c_hi, NT)
+        total = total * (4.0 / O)
+        pb[2 * q] = pb[2 * q] + total[:, 0:128]
+        pb[2 * q + 1] = pb[2 * q + 1] + total[:, 128:256]
+
+    for q in range(4):
+        x_decode(z, q)
+
+    @pl.loop(1, 8)
+    def _(t):
+        lo_s, hi_s = z - t, z + t
+        for q in range(4):
+            @pl.when(lo_s >= 0)
+            def _():
+                x_out(0, lo_s, q, up).wait_recv()
+                pl.when(z < 7)(lambda: x_out(0, lo_s, q, up).start())
+
+            @pl.when(hi_s <= 7)
+            def _():
+                x_out(1, hi_s, q, down).wait_recv()
+                pl.when(z > 0)(lambda: x_out(1, hi_s, q, down).start())
+
+            pl.when(lo_s >= 0)(lambda: x_decode(lo_s, q))
+            pl.when(hi_s <= 7)(lambda: x_decode(hi_s, q))
+            pl.when(lo_s + 1 >= 0)(lambda: p_add(lo_s + 1, q))
+            pl.when(jnp.logical_and(t > 1, hi_s - 1 <= 7))(lambda: p_add(hi_s - 1, q))
+
+        @pl.when(t == 2)
+        def _():
+            for zz in zpeer:
+                f_2_in(zz).wait_recv()
+            for cc in cpeer:
+                f_3(cc).start()
+            fa3[c] = fag[c]
+
+    for q in range(4):
+        pl.when(z == 7)(lambda: p_add(0, q))
+        pl.when(z == 0)(lambda: p_add(7, q))
 
     def cols(h):
         return pl.ds(h * 256, 256)
@@ -351,20 +334,9 @@
             n_y(h, yy).start()
         n_c(h, y).start()
 
-    x_step(0, 0)
-    x_step(1, 0)
-    x_step(0, 1)
-    x_step(2, 0)
-    x_step(1, 1)
-    x_step(3, 0)
-    left_factors()
-    x_step(2, 1)
-    x_mate(3, 0)
     p_core(0)
-    x_step(3, 1)
+    p_core(1)
     p_plane(0)
-    x_mate(3, 1)
-    p_core(1)
     p_plane(1)
     p_end(0)
     p_end(1)
@@ -429,10 +401,6 @@
         n_far(ypeer[2], h)
         f_add(ypeer[2], h)
 
-    def z_mate(d, q):
-        rows = pl.ds(q * 128, 128)
-        return rc(zms.at[d, rows], zmr.at[d, rows], zm_s.at[d, q], zm_r.at[d, q], mate, c)
-
     def z_out(direction, d, q, zz):
         rows = pl.ds(q * 128, 128)
         return rc(
@@ -440,80 +408,76 @@
             zr_s.at[direction, d, q], zr_r.at[direction, d, q], zz, c,
         )
 
-    def z_start(h):
-        for k in range(4):
-            d = 2 * lax.select(m < 2, 3 - k, k) + 1 - par
-            for q in (2 * h, 2 * h + 1):
-                rows = pl.ds(q * 128, 128)
-                zms[d, rows] = enc(fb[d, rows])
-                z_mate(d, q).start()
-
-    def z_pass(direction, d, h, first, zz):
+    def z_move(direction, d, q, first, last, zz):
+        rows = pl.ds(q * 128, 128)
+
+        @pl.when(jnp.logical_and(first, jnp.logical_not(last)))
+        def _():
+            zs[direction, d, rows] = enc(fb[d, rows])
+
+        @pl.when(jnp.logical_not(first))
+        def _():
+            z_out(direction, d, q, zz).wait_recv()
+            total = fb[d, rows] + dec(zr[direction, d, rows])
+
+            @pl.when(last)
+            def _():
+                fb[d, rows] = total
+
+            @pl.when(jnp.logical_not(last))
+            def _():
+                zs[direction, d, rows] = enc(total)
+
+        @pl.when(jnp.logical_not(last))
+        def _():
+            z_out(direction, d, q, zz).start()
+
+    def z_step(t, h):
         for q in (2 * h, 2 * h + 1):
-            rows = pl.ds(q * 128, 128)
-            z_mate(d, q).wait_recv()
-
-            @pl.when(first)
-            def _():
-                zs[direction, d, rows] = enc(fb[d, rows] + dec(zmr[d, rows]))
-
-            @pl.when(jnp.logical_not(first))
-            def _():
-                z_out(direction, d, q, zz).wait_recv()
-                zs[direction, d, rows] = enc(fb[d, rows] + dec(zmr[d, rows]) + dec(zr[direction, d, rows]))
-
-            z_out(direction, d, q, zz).start()
-
-    def z_step(t, h):
-        pl.when(t >= m)(lambda: z_pass(0, 2 * (3 + m - t) + par, h, m == 0, up))
-        pl.when(t >= 3 - m)(lambda: z_pass(1, 2 * (t - 3 + m) + par, h, m == 3, down))
-
-    def z_end(h):
-        for q in (2 * h, 2 * h + 1):
-            rows = pl.ds(q * 128, 128)
-            z_mate(z, q).wait_recv()
-            fb[z, rows] = fb[z, rows] + dec(zmr[z, rows])
-
-            @pl.when(m > 0)
-            def _():
-                z_out(0, z, q, up).wait_recv()
-                fb[z, rows] = fb[z, rows] + dec(zr[0, z, rows])
-
-            @pl.when(m < 3)
-            def _():
-                z_out(1, z, q, down).wait_recv()
-                fb[z, rows] = fb[z, rows] + dec(zr[1, z, rows])
-
-    second(0)
-    z_start(0)
-    second(1)
-    tz[z] = nag[z, c]
-    z_start(1)
-    z_step(0, 0)
-    z_step(1, 0)
-    z_step(0, 1)
-    z_step(2, 0)
-    z_step(1, 1)
-    for zz in zpeer:
-        t_z_in(zz).wait_recv()
-    for r in cpeer:
-        t_n(r).start()
-    tn[c] = tz[c]
-    z_end(0)
-    z_step(2, 1)
-    for r in cpeer:
-        t_n_in(r).wait_recv()
-    rows_a = dec(tn[...].reshape(C2, 128)).T
-    hi, lo = split(rows_a)
-    lo2 = (rows_a - hi.astype(F32) - lo.astype(F32)).astype(BF)
-    back = (lax.broadcasted_iota(jnp.int32, shape_sq, 0) == source_column(lax.broadcasted_iota(jnp.int32, shape_sq, 1))).astype(F32).astype(BF)
-    na_ref[...] = dot(hi, back, NT) + dot(lo, back, NT) + dot(lo2, back, NT)
-    for k in range(2):
+            pl.when(t >= z)(lambda: z_move(0, 7 + z - t, q, z == 0, t == 7, up))
+            pl.when(t >= 7 - z)(lambda: z_move(1, t - 7 + z, q, z == 7, t == 7, down))
+
+    def natural():
+        rows_a = dec(tn[...].reshape(C2, 128)).T
+        hi, lo = split(rows_a)
+        return rows_a, hi, lo
+
+    def second_difference(k):
+        _, hi, lo = natural()
         hi_k = jnp.where(lane_k == k, hi.astype(F32), 0.0).astype(BF)
         lo_k = jnp.where(lane_k == k, lo.astype(F32), 0.0).astype(BF)
         fit = dot(hi_k, ball[...]) + dot(lo_k, ball[...])
         d2[k * 128:(k + 1) * 128, :] = (wk[k].astype(F32) - fit).astype(BF)
-    z_end(1)
+
+    second(0)
+    z_step(0, 0)
+    second(1)
+    tz[z] = nag[z, c]
+
+    @pl.loop(0, 7)
+    def _(t):
+        z_step(t + 1, 0)
+        z_step(t, 1)
+
+        @pl.when(t == 3)
+        def _():
+            for zz in zpeer:
+                t_z_in(zz).wait_recv()
+            for r in cpeer:
+                t_n(r).start()
+            tn[c] = tz[c]
+
+        @pl.when(t == 5)
+        def _():
+            for r in cpeer:
+                t_n_in(r).wait_recv()
+            second_difference(0)
+
+        @pl.when(t == 6)
+        def _():
+            second_difference(1)
+
+    z_step(7, 1)
 
     field = fb[z] * (FIELD_UP * 8.0 / D)
     wide = jnp.concatenate([jnp.where(sub_k == 0, field, 0.0), jnp.where(sub_k == 1, field, 0.0)], axis=1)
@@ -550,6 +514,10 @@
         for yy in ypeer:
             fys[h, yy] = enc(p2[h, yy] + dec(fcr[h, yy]))
             f_y(h, yy).start()
+    rows_a, hi, lo = natural()
+    lo2 = (rows_a - hi.astype(F32) - lo.astype(F32)).astype(BF)
+    back = (lax.broadcasted_iota(jnp.int32, shape_sq, 0) == source_column(lax.broadcasted_iota(jnp.int32, shape_sq, 1))).astype(F32).astype(BF)
+    na_ref[...] = dot(hi, back, NT) + dot(lo, back, NT) + dot(lo2, back, NT)
     for h in range(2):
         total = p2[h, y] + dec(fcr[h, y])
         for yy in ypeer:
@@ -595,16 +563,13 @@
     for h in range(2):
         f_c(h).wait_send()
 
-    @pl.loop(0, 4)
-    def _(e):
-        s = 2 * e + par
+    @pl.loop(0, 8)
+    def _(s):
         for q in range(4):
-            pl.when(jnp.logical_and(e <= m, m < 3))(lambda: x_out(0, s, q, up).wait_send())
-            pl.when(jnp.logical_and(e >= m, m > 0))(lambda: x_out(1, s, q, down).wait_send())
-            x_out(2, s, q, mate).wait_send()
-            z_mate(2 * e + 1 - par, q).wait_send()
-            pl.when(e > m)(lambda: z_out(0, s, q, up).wait_send())
-            pl.when(e < m)(lambda: z_out(1, s, q, down).wait_send())
+            pl.when(jnp.logical_and(s <= z, z < 7))(lambda: x_out(0, s, q, up).wait_send())
+            pl.when(jnp.logical_and(s >= z, z > 0))(lambda: x_out(1, s, q, down).wait_send())
+            pl.when(s > z)(lambda: z_out(0, s, q, up).wait_send())
+            pl.when(s < z)(lambda: z_out(1, s, q, down).wait_send())
 
 
 def per_device(covariance, weight, factor_a, factor_b):
@@ -644,8 +609,6 @@
             pltpu.VMEM((8, 64, 128), BF),
             pltpu.VMEM((8, 64, 128), BF),
             pltpu.VMEM(blk, F32),
-            pltpu.VMEM(blk, BF),
-            pltpu.VMEM(blk, BF),
             pltpu.VMEM((2,) + blk, BF),
             pltpu.VMEM((2,) + blk, BF),
             pltpu.VMEM((256, O), BF),
@@ -660,15 +623,15 @@
             dma, dma,
             dma((8,)), dma((8,)), dma((4, 8)), dma((4, 8)), dma((4,)), dma((4,)),
             dma((8,)), dma((8,)), dma((8,)), dma((8,)), dma((8,)), dma((8,)),
-            dma((3, 8, 4)), dma((8, 4)),
+            dma((2, 8, 4)), dma((8, 4)),
             dma((2, 4)), dma((2, 4)), dma((2, 4)), dma((2, 4)),
             dma((2, 4)), dma((2, 4)), dma((2, 8)),
             dma((8,)), dma((8,)), dma((8,)), dma((8,)),
-            dma((8, 4)), dma((8, 4)), dma((2, 8, 4)), dma((2, 8, 4)),
+            dma((2, 8, 4)), dma((2, 8, 4)),
             dma((2,)), dma((2,)), dma((2, 4)), dma((2, 4)), dma((2, 8)), dma((2, 8)),
         ],
         compiler_params=pltpu.CompilerParams(
-            collective_id=0, has_side_effects=True, vmem_limit_bytes=52 * 2**20
+            collective_id=0, has_side_effects=True, vmem_limit_bytes=56 * 2**20
         ),
     )(covariance, weight, factor_a, factor_b)
     return new_a.reshape(n, 2, R), new_b.reshape(2, 4, O)

time: 136 us -> 130 us (0.956)
  Pallas kernels: 131 us -> 126 us
    pallas_call x1, Pallas kernels: 131 us -> 126 us  [per_device(): pl.pallas_call(kernel, name='refine', out_shape=(jax.ShapeDtypeStruct((n,...]
    unnamed x6 -> x0, local copies, waits for them, and re-layouts: 2.66 us -> none
    reshape x2, local copies, waits for them, and re-layouts: 1.49 us -> 3.2 us  [per_device(): return (new_a.reshape(n, 2, R), new_b.reshape(2, 4, O))]
where the time goes in v4:
time: 130 us; the launch traced here: 129 us
  Pallas kernels  126 us (97%)
  local copies, waits for them, and re-layouts  3.2 us (2%)
    pallas_call x1, Pallas kernels, per_device(): pl.pallas_call(kernel, name='refine', out_shape=(jax.ShapeDtypeStruct((n,...  126 us
    reshape x2, local copies, waits for them, and re-layouts, per_device(): return (new_a.reshape(n, 2, R), new_b.reshape(2, 4, O))  3.2 us

profile of v4, /device:TPU:1, one launch (start us, length us, event | category | flops | bytes accessed | tf_op | source)
XLA Modules:
  0.0 129.4 jit_solution(13890894894623387958)
XLA Ops:
  0.6 125.6 %refine.1 = (f32[128,512]{1,0:T(8,128)}, f32[8,1024]{1,0:T(8,128)}) custom-call(f32[1024,1024]{1,0:T(8,128)} %cov_hbm.1, bf16[128,2,1024]{2,1,0:T(2,128)(2,1)} %w_hbm.1, bf16[128,2,256]{2,1,0:T(2,128)(2,1)} %a_ref.1, bf16[2,4,1024]{2,1,0:T(4,128)(2,1)} %b_ref.1), custom_call_target="tpu_custom_call" | custom-call | tf_op jit(solution)/shard_map/refine/pallas_call | solution.py:580
  126.2 1.8 %reshape.10 = f32[128,2,256]{2,1,0:T(2,128)} reshape(f32[128,512]{1,0:T(8,128)} %get-tuple-element.4) | data formatting | bytes 524288 | tf_op jit(solution)/shard_map/reshape | solution.py:637
  128.0 1.4 %reshape.11 = f32[2,4,1024]{2,1,0:T(4,128)} reshape(f32[8,1024]{1,0:T(8,128)} %get-tuple-element.5) | data formatting | bytes 65536 | tf_op jit(solution)/shard_map/reshape | solution.py:637

commit v5 on v4

--- a/solution.py
+++ b/solution.py
@@ -51,10 +51,10 @@
 
 
 def kernel(
-    cov_hbm, w_hbm, a_ref, b_ref, na_ref, nb_ref,
-    cov, wv, wk, chi, clo, ccat, gat, ball, aint, xg, xh, xl, fas, fa1, fag, fa3, pb, pes, per_, ses, ser,
+    cov_hbm, w_hbm, a_hbm, b_ref, na_ref, nb_ref,
+    cov, wv, av, wk, chi, clo, ccat, gat, ball, aint, xg, xh, xl, fas, fa1, fag, fa3, pb, pes, per_, ses, ser,
     nag, tz, tn, fb, zs, zr, d2, p2, fcs, fcr, fys, fyr, fsum, fzs, fzr,
-    cov_sem, w_sem, bz_s, bz_r, by_s, by_r, bc_s, bc_r, f1_s, f1_r, f2_s, f2_r, f3_s, f3_r, xg_s, xg_r,
+    cov_sem, w_sem, a_sem, bz_s, bz_r, by_s, by_r, bc_s, bc_r, f1_s, f1_r, f2_s, f2_r, f3_s, f3_r, xg_s, xg_r,
     pc_s, pc_r, ps_s, ps_r, ny_s, nc_s, ng_r, tz_s, tz_r, tn_s, tn_r, zr_s, zr_r,
     fc_s, fc_r, fy_s, fy_r, fz_s, fz_r,
 ):
@@ -74,6 +74,8 @@
 
     cov_copy = pltpu.make_async_copy(cov_hbm, cov, cov_sem)
     w_copy = pltpu.make_async_copy(w_hbm, wv, w_sem)
+    a_copy = pltpu.make_async_copy(a_hbm, av, a_sem)
+    a_copy.start()
     cov_copy.start()
     w_copy.start()
 
@@ -91,58 +93,59 @@
     b_own = jnp.concatenate([b_own[0], b_own[1]], axis=0)
     gat[core, y, z] = jnp.concatenate([b_own[:, 0:512], b_own[:, 512:1024]], axis=0).astype(BF)
 
+    pl.semaphore_wait(barrier, 14)
+
+    def b_z(zz):
+        return rc(gat.at[core, y, z], gat.at[core, y, z], bz_s.at[zz], bz_r.at[z], zz, c)
+
+    def b_z_in(zz):
+        return rc(gat.at[core, y, zz], gat.at[core, y, zz], bz_s.at[zz], bz_r.at[zz], zz, c)
+
+    def b_y(yy, zz):
+        return rc(gat.at[core, y, zz], gat.at[core, y, zz], by_s.at[yy, zz], by_r.at[y, zz], z, 2 * yy + core)
+
+    def b_y_in(yy, zz):
+        return rc(gat.at[core, yy, zz], gat.at[core, yy, zz], by_s.at[yy, zz], by_r.at[yy, zz], z, 2 * yy + core)
+
+    def b_c(yy):
+        return rc(gat.at[core, yy], gat.at[core, yy], bc_s.at[yy], bc_r.at[yy], z, other)
+
+    def b_c_in(yy):
+        return rc(gat.at[1 - core, yy], gat.at[1 - core, yy], bc_s.at[yy], bc_r.at[yy], z, other)
+
+    for zz in zpeer:
+        b_z(zz).start()
+    for yy in ypeer:
+        b_y(yy, z).start()
+
+    def f_1(cc):
+        return rc(fas.at[cc], fa1.at[c], f1_s.at[cc], f1_r.at[c], z, cc)
+
+    def f_1_in(cc):
+        return rc(fas.at[cc], fa1.at[cc], f1_s.at[cc], f1_r.at[cc], z, cc)
+
+    def f_2(zz):
+        return rc(fa1.at[zz], fag.at[z], f2_s.at[zz], f2_r.at[z], zz, c)
+
+    def f_2_in(zz):
+        return rc(fa1.at[zz], fag.at[zz], f2_s.at[zz], f2_r.at[zz], zz, c)
+
+    def f_3(cc):
+        return rc(fag.at[cc], fa3.at[c], f3_s.at[cc], f3_r.at[c], z, cc)
+
+    def f_3_in(cc):
+        return rc(fag.at[cc], fa3.at[cc], f3_s.at[cc], f3_r.at[cc], z, cc)
+
     shape_sq = (C2, C2)
     row_sq = lax.broadcasted_iota(jnp.int32, shape_sq, 0)
     col_sq = lax.broadcasted_iota(jnp.int32, shape_sq, 1)
     unmix = (row_sq == source_column(col_sq)).astype(F32).astype(BF)
     unmix_t = (col_sq == source_column(row_sq)).astype(F32).astype(BF)
-    a_all = a_ref[...].astype(F32)
+    a_copy.wait()
+    a_all = av[...].astype(F32)
     a_flat = jnp.concatenate([a_all[:, 0, :], a_all[:, 1, :]], axis=1).astype(BF)
     aint[...] = dot(a_flat, unmix).astype(BF)
     fas[...] = dot(unmix_t, a_flat, NT).astype(BF).reshape(8, 64, 128)
-
-    pl.semaphore_wait(barrier, 14)
-
-    def b_z(zz):
-        return rc(gat.at[core, y, z], gat.at[core, y, z], bz_s.at[zz], bz_r.at[z], zz, c)
-
-    def b_z_in(zz):
-        return rc(gat.at[core, y, zz], gat.at[core, y, zz], bz_s.at[zz], bz_r.at[zz], zz, c)
-
-    def b_y(yy, zz):
-        return rc(gat.at[core, y, zz], gat.at[core, y, zz], by_s.at[yy, zz], by_r.at[y, zz], z, 2 * yy + core)
-
-    def b_y_in(yy, zz):
-        return rc(gat.at[core, yy, zz], gat.at[core, yy, zz], by_s.at[yy, zz], by_r.at[yy, zz], z, 2 * yy + core)
-
-    def b_c(yy):
-        return rc(gat.at[core, yy], gat.at[core, yy], bc_s.at[yy], bc_r.at[yy], z, other)
-
-    def b_c_in(yy):
-        return rc(gat.at[1 - core, yy], gat.at[1 - core, yy], bc_s.at[yy], bc_r.at[yy], z, other)
-
-    for zz in zpeer:
-        b_z(zz).start()
-    for yy in ypeer:
-        b_y(yy, z).start()
-
-    def f_1(cc):
-        return rc(fas.at[cc], fa1.at[c], f1_s.at[cc], f1_r.at[c], z, cc)
-
-    def f_1_in(cc):
-        return rc(fas.at[cc], fa1.at[cc], f1_s.at[cc], f1_r.at[cc], z, cc)
-
-    def f_2(zz):
-        return rc(fa1.at[zz], fag.at[z], f2_s.at[zz], f2_r.at[z], zz, c)
-
-    def f_2_in(zz):
-        return rc(fa1.at[zz], fag.at[zz], f2_s.at[zz], f2_r.at[zz], zz, c)
-
-    def f_3(cc):
-        return rc(fag.at[cc], fa3.at[c], f3_s.at[cc], f3_r.at[c], z, cc)
-
-    def f_3_in(cc):
-        return rc(fag.at[cc], fa3.at[cc], f3_s.at[cc], f3_r.at[cc], z, cc)
 
     for cc in cpeer:
         f_1(cc).start()
@@ -163,14 +166,23 @@
             ccat[rows, s * 256 + 128:(s + 1) * 256] = lo[:, s * 128:(s + 1) * 128]
         pb[i] = jnp.zeros((C2, 128), F32)
 
+    def w_split(i):
+        rows = pl.ds(pl.multiple_of(i * 16, 16), 16)
+        piece = wv[rows].astype(F32)
+        wk[0, rows, :] = piece[:, 0, :].astype(BF)
+        wk[1, rows, :] = piece[:, 1, :].astype(BF)
+
     cov_copy.wait()
+    w_copy.wait()
     cov_split(0)
+    w_split(0)
 
     @pl.loop(1, 8)
     def _(t):
         pl.when(z - t >= 0)(lambda: b_forward(z - t))
         pl.when(z + t <= 7)(lambda: b_forward(z + t))
         cov_split(t)
+        w_split(t)
 
     b_c(y).start()
 
@@ -191,15 +203,6 @@
         ball[rows, 512:1024] = both[64:128]
 
     unpack(core, y)
-    w_copy.wait()
-
-    @pl.loop(0, 8)
-    def _(i):
-        rows = pl.ds(pl.multiple_of(i * 16, 16), 16)
-        piece = wv[rows].astype(F32)
-        wk[0, rows, :] = piece[:, 0, :].astype(BF)
-        wk[1, rows, :] = piece[:, 1, :].astype(BF)
-
     for yy in ypeer:
         for zz in zpeer + [z]:
             b_y_in(yy, zz).wait_recv()
@@ -581,11 +584,12 @@
         kernel,
         name="refine",
         out_shape=(jax.ShapeDtypeStruct((n, C2), F32), jax.ShapeDtypeStruct((8, O), F32)),
-        in_specs=[pl.BlockSpec(memory_space=pl.ANY), pl.BlockSpec(memory_space=pl.ANY), vm, vm],
+        in_specs=[pl.BlockSpec(memory_space=pl.ANY)] * 3 + [vm],
         out_specs=(vm, vm),
         scratch_shapes=[
             pltpu.VMEM((1024, 1024), F32),
             pltpu.VMEM((n, 2, O), BF),
+            pltpu.VMEM((n, 2, R), BF),
             pltpu.VMEM((2, n, O), BF),
             pltpu.VMEM((1024, 1024), BF),
             pltpu.VMEM((1024, 1024), BF),
@@ -620,7 +624,7 @@
             pltpu.VMEM((2, 8, 8, 512), F32),
             pltpu.VMEM((2, 8, 16, 256), BF),
             pltpu.VMEM((2, 8, 16, 256), BF),
-            dma, dma,
+            dma, dma, dma,
             dma((8,)), dma((8,)), dma((4, 8)), dma((4, 8)), dma((4,)), dma((4,)),
             dma((8,)), dma((8,)), dma((8,)), dma((8,)), dma((8,)), dma((8,)),
             dma((2, 8, 4)), dma((8, 4)),

time: 130 us -> 130 us (level)
  no operation moved by 1% of the time
where the time goes in v5:
time: 130 us; the launch traced here: 129 us
  Pallas kernels  126 us (97%)
  local copies, waits for them, and re-layouts  3.2 us (2%)
    pallas_call x1, Pallas kernels, per_device(): pl.pallas_call(kernel, name='refine', out_shape=(jax.ShapeDtypeStruct((n,...  126 us
    reshape x2, local copies, waits for them, and re-layouts, per_device(): return (new_a.reshape(n, 2, R), new_b.reshape(2, 4, O))  3.2 us

profile of v5, /device:TPU:1, one launch (start us, length us, event | category | flops | bytes accessed | tf_op | source)
XLA Modules:
  0.0 129.4 jit_solution(10107130351665995948)
XLA Ops:
  0.6 125.6 %refine.1 = (f32[128,512]{1,0:T(8,128)}, f32[8,1024]{1,0:T(8,128)}) custom-call(f32[1024,1024]{1,0:T(8,128)} %cov_hbm.1, bf16[128,2,1024]{2,1,0:T(2,128)(2,1)} %w_hbm.1, bf16[128,2,256]{2,1,0:T(2,128)(2,1)} %a_hbm.1, bf16[2,4,1024]{2,1,0:T(4,128)(2,1)} %b_ref.1), custom_call_target="tpu_custom_call" | custom-call | tf_op jit(solution)/shard_map/refine/pallas_call | solution.py:583
  126.2 1.8 %reshape.10 = f32[128,2,256]{2,1,0:T(2,128)} reshape(f32[128,512]{1,0:T(8,128)} %get-tuple-element.4) | data formatting | bytes 524288 | tf_op jit(solution)/shard_map/reshape | solution.py:641
  128.0 1.4 %reshape.11 = f32[2,4,1024]{2,1,0:T(4,128)} reshape(f32[8,1024]{1,0:T(8,128)} %get-tuple-element.5) | data formatting | bytes 65536 | tf_op jit(solution)/shard_map/reshape | solution.py:641

commit v6 on v5

--- a/solution.py
+++ b/solution.py
@@ -250,10 +250,24 @@
         pb[2 * q] = pb[2 * q] + total[:, 0:128]
         pb[2 * q + 1] = pb[2 * q + 1] + total[:, 128:256]
 
+    def p_rows(s, q):
+        rows = pl.ds(q * 128, 128)
+        lanes = pl.ds(pl.multiple_of(s * 128, 128), 128)
+        wide = pl.ds(pl.multiple_of(s * 256, 256), 256)
+        hi = xh[rows, lanes]
+        both = jnp.concatenate([hi, hi], axis=1)
+        low = xl[rows, lanes]
+        for i in range(4):
+            part = pl.ds(i * 256, 256)
+            total = dot(both, ccat[part, wide], NT) + dot(low, chi[part, lanes], NT)
+            total = total * (4.0 / O)
+            pb[2 * i, rows] = pb[2 * i, rows] + total[:, 0:128]
+            pb[2 * i + 1, rows] = pb[2 * i + 1, rows] + total[:, 128:256]
+
     for q in range(4):
         x_decode(z, q)
 
-    @pl.loop(1, 8)
+    @pl.loop(1, 7)
     def _(t):
         lo_s, hi_s = z - t, z + t
         for q in range(4):
@@ -281,8 +295,15 @@
             fa3[c] = fag[c]
 
     for q in range(4):
-        pl.when(z == 7)(lambda: p_add(0, q))
-        pl.when(z == 0)(lambda: p_add(7, q))
+        pl.when(z >= 6)(lambda: p_add(z - 6, q))
+        pl.when(z <= 1)(lambda: p_add(z + 6, q))
+
+    def x_last(q):
+        @pl.when(jnp.logical_or(z == 0, z == 7))
+        def _():
+            x_out(0, 7 - z, q, up).wait_recv()
+            x_decode(7 - z, q)
+            p_rows(7 - z, q)
 
     def cols(h):
         return pl.ds(h * 256, 256)
@@ -337,9 +358,13 @@
             n_y(h, yy).start()
         n_c(h, y).start()
 
+    x_last(0)
+    x_last(1)
     p_core(0)
+    x_last(2)
+    p_plane(0)
+    x_last(3)
     p_core(1)
-    p_plane(0)
     p_plane(1)
     p_end(0)
     p_end(1)

time: 130 us -> 128 us (0.985)
  Pallas kernels: 126 us -> 124 us
    pallas_call x1, Pallas kernels: 126 us -> 124 us  [per_device(): pl.pallas_call(kernel, name='refine', out_shape=(jax.ShapeDtypeStruct((n,...]
where the time goes in v6:
time: 128 us; the launch traced here: 127 us
  Pallas kernels  124 us (97%)
  local copies, waits for them, and re-layouts  3.2 us (2%)
    pallas_call x1, Pallas kernels, per_device(): pl.pallas_call(kernel, name='refine', out_shape=(jax.ShapeDtypeStruct((n,...  124 us
    reshape x2, local copies, waits for them, and re-layouts, per_device(): return (new_a.reshape(n, 2, R), new_b.reshape(2, 4, O))  3.2 us

profile of v6, /device:TPU:1, one launch (start us, length us, event | category | flops | bytes accessed | tf_op | source)
XLA Modules:
  0.0 127.5 jit_solution(17145490889888872340)
XLA Ops:
  0.6 123.6 %refine.1 = (f32[128,512]{1,0:T(8,128)}, f32[8,1024]{1,0:T(8,128)}) custom-call(f32[1024,1024]{1,0:T(8,128)} %cov_hbm.1, bf16[128,2,1024]{2,1,0:T(2,128)(2,1)} %w_hbm.1, bf16[128,2,256]{2,1,0:T(2,128)(2,1)} %a_hbm.1, bf16[2,4,1024]{2,1,0:T(4,128)(2,1)} %b_ref.1), custom_call_target="tpu_custom_call" | custom-call | tf_op jit(solution)/shard_map/refine/pallas_call | solution.py:608
  124.3 1.8 %reshape.10 = f32[128,2,256]{2,1,0:T(2,128)} reshape(f32[128,512]{1,0:T(8,128)} %get-tuple-element.4) | data formatting | bytes 524288 | tf_op jit(solution)/shard_map/reshape | solution.py:666
  126.1 1.4 %reshape.11 = f32[2,4,1024]{2,1,0:T(4,128)} reshape(f32[8,1024]{1,0:T(8,128)} %get-tuple-element.5) | data formatting | bytes 65536 | tf_op jit(solution)/shard_map/reshape | solution.py:666
